TPU v7x, 32 devices: a whole 2x2x4 slice. The times are simulated.
32 devices in a mesh: seq: 8 (over y, x, core), head: 4 (over z).
Axes of the slice: x: 2, y: 2, z: 4, core: 2. Of those that a mesh axis runs over, the one named last changes fastest.
Arguments:
- tokens: bfloat16 [16, 512, 1024], P('seq', 'head'), may hold values from -6 to 6
- doc_lengths: int32 [16, 3], P('seq'), may hold values from 1 to 128, as said below
- pad_counts: int32 [16], P('seq'), may hold values from 0 to 64
- w_query: bfloat16 [1024, 1024], replicated, may hold values from -0.1875 to 0.1875
- w_key: bfloat16 [1024, 1024], replicated, may hold values from -0.1875 to 0.1875
- w_value: bfloat16 [1024, 1024], replicated, may hold values from -0.1875 to 0.1875
- w_out: bfloat16 [1024, 1024], replicated, may hold values from -2 to 2
- w_inner: bfloat16 [1024, 4096], replicated, may hold values from -0.1875 to 0.1875
- w_outer: bfloat16 [4096, 1024], replicated, may hold values from -0.09375 to 0.09375
- bias_query: float32 [1024], replicated, may hold values from -3 to 3
- bias_value: float32 [1024], replicated, may hold values from -3 to 3
- bias_out: float32 [1024], replicated, may hold values from -3 to 3
- bias_inner: float32 [4096], replicated, may hold values from -3 to 3
- bias_outer: float32 [1024], replicated, may hold values from -3 to 3
- gain_attn: float32 [1024], replicated, may hold values from 0.5 to 1.5
- beta_attn: float32 [1024], replicated, may hold values from -3 to 3
- gain_final: float32 [1024], replicated, may hold values from 0.5 to 1.5
- beta_final: float32 [1024], replicated, may hold values from -3 to 3
- cotangent: bfloat16 [16, 512, 1024], P('seq', 'head'), may hold values from -6 to 6
Outputs:
- layer_out: bfloat16 [16, 512, 1024], P('seq', 'head')
- input_grad: float32 [16, 512, 1024], P('seq', 'head')
- grad_bias_query: float32 [1024], replicated
- grad_bias_value: float32 [1024], replicated
- grad_bias_out: float32 [1024], replicated
- grad_bias_inner: float32 [4096], replicated
- grad_bias_outer: float32 [1024], replicated
- grad_beta_attn: float32 [1024], replicated
- grad_beta_final: float32 [1024], replicated
Inputs may be any that keep to these rules, and one draw needn't show every extreme that they name: `doc_lengths`: lengths of the first 3 documents of a row, in order; the row's last document takes the remaining slots before its padding.
All inputs are finite; a program needn't handle non-finite values.
Results may differ from a plain program's by a relative error of at most 0.012.
Values may be sent and summed in bfloat16 or wider, within the bound.
A program may use at most 128 MiB of HBM per device.

v0:
```python
import functools

import jax
import jax.numpy as jnp
from jax import lax
from jax.experimental import pallas as pl
from jax.experimental.pallas import tpu as pltpu
from jax.sharding import PartitionSpec as P

HEADS = 16
LANES = 128
EPS = 1e-06
BIG = 2.0**30
FF_CHUNK = 512
NORM_ROWS = 32
MESH = pl.DeviceIdType.MESH
F32 = jnp.float32
BF16 = jnp.bfloat16


def dot(left, right):
    return lax.dot_general(left, right, (((1,), (0,)), ((), ())), preferred_element_type=F32)


def dot_nt(left, right):
    return lax.dot_general(left, right, (((1,), (1,)), ((), ())), preferred_element_type=F32)


def dot_tn(left, right):
    return lax.dot_general(left, right, (((0,), (0,)), ((), ())), preferred_element_type=F32)


def normed(hidden):
    row_mean = jnp.mean(hidden, axis=-1, keepdims=True)
    centred = hidden - row_mean
    inv_std = lax.rsqrt(jnp.mean(centred * centred, axis=-1, keepdims=True) + EPS)
    return centred * inv_std, inv_std


def norm_back(gradient, norm, inv_std):
    return inv_std * (
        gradient
        - jnp.mean(gradient, axis=-1, keepdims=True)
        - norm * jnp.mean(gradient * norm, axis=-1, keepdims=True)
    )


def fold_rows(block):
    total = block[0:8]
    for start in range(8, block.shape[0], 8):
        total = total + block[start : start + 8]
    return total


def kernel(
    seq_size,
    group,
    tokens,
    cotangent,
    doc_lengths,
    pad_counts,
    w_query,
    w_key,
    w_value,
    w_out,
    w_inner,
    w_outer,
    bias_query,
    bias_value,
    bias_out,
    bias_inner,
    bias_outer,
    gain_attn,
    beta_attn,
    gain_final,
    beta_final,
    layer_home,
    grad_home,
    sums_a,
    sums_b,
    m_qkv,
    m_out,
    m_inner,
    m_outer,
    row,
    cot,
    info,
    qs,
    ks,
    vs,
    exps,
    recip,
    mixed,
    att,
    att_far,
    norm_a,
    inv_a,
    mid,
    mid_low,
    acc,
    slope,
    grad_h,
    grad_low,
    grad_att,
    grad_far,
    grad_qkv,
    part_out,
    part_in,
    grad_out,
    layer_out,
    pool_a,
    z_a,
    pool_b,
    z_b,
    w_sem,
    in_sem,
    tok_send,
    tok_recv,
    pass_send,
    pass_recv,
    info_sem,
    cot_send,
    cot_recv,
    att_send,
    att_recv,
    gat_send,
    gat_recv,
    lay_send,
    lay_recv,
    part_sem,
    grad_send,
    grad_recv,
    pa_send,
    pa_recv,
    za_send,
    za_recv,
    pb_send,
    pb_recv,
    zb_send,
    zb_recv,
):
    rows, span, width = tokens.shape
    half_blocks = group // 2
    slots = span * group
    half = slots // 2
    head_width = width // HEADS
    side = width // 2
    pairs = side // LANES
    chunks = m_inner.shape[0]
    score_scale = head_width**-0.5

    seq = lax.axis_index("seq")
    z = lax.axis_index("head")
    core = lax.rem(seq, 2)
    base = seq - core
    partner = base + 1 - core
    z_half = z // half_blocks
    far = 1 - core

    def rows_of(block):
        return pl.ds(pl.multiple_of(block * span, span), span)

    def remote(src, dst, send_sem, recv_sem, at_seq, at_head):
        return pltpu.make_async_remote_copy(
            src_ref=src,
            dst_ref=dst,
            send_sem=send_sem,
            recv_sem=recv_sem,
            device_id=(at_seq, at_head),
            device_id_type=MESH,
        )

    barrier = pltpu.get_barrier_semaphore()

    def greet_z(step, carry):
        pl.semaphore_signal(
            barrier, inc=1, device_id=(seq, lax.rem(z + step, group)), device_id_type=MESH
        )
        return carry

    def greet_seq(step, carry):
        pl.semaphore_signal(
            barrier, inc=1, device_id=(lax.rem(seq + step, seq_size), z), device_id_type=MESH
        )
        return carry

    for r in range(rows):
        target = core * rows + r

        @pl.when(target != z)
        def _():
            pl.semaphore_signal(
                barrier, inc=1, device_id=(base + z_half, target), device_id_type=MESH
            )

    lax.fori_loop(1, seq_size, greet_seq, 0)
    lax.fori_loop(1, group, greet_z, 0)

    mine = pl.ds(pl.multiple_of(core * side, side), side)
    theirs = pl.ds(pl.multiple_of(far * side, side), side)
    qkv_copies = [
        pltpu.make_async_copy(
            weight.at[:, mine], m_qkv.at[:, i * side : (i + 1) * side], w_sem.at[i]
        )
        for i, weight in enumerate((w_query, w_key, w_value))
    ]
    for copy in qkv_copies:
        copy.start()
    out_copies = [
        pltpu.make_async_copy(w_out.at[mine], m_out.at[0:side], w_sem.at[3]),
        pltpu.make_async_copy(w_out.at[theirs], m_out.at[side:width], w_sem.at[4]),
    ]

    def inner_copy(f):
        columns = pl.ds(pl.multiple_of(f * FF_CHUNK, FF_CHUNK), FF_CHUNK)
        return pltpu.make_async_copy(w_inner.at[:, columns], m_inner.at[f], w_sem.at[5 + f])

    def outer_copy(f):
        lines = pl.ds(pl.multiple_of(f * FF_CHUNK, FF_CHUNK), FF_CHUNK)
        return pltpu.make_async_copy(w_outer.at[lines], m_outer.at[f], w_sem.at[5 + chunks + f])

    line = lax.broadcasted_iota(jnp.int32, (8, LANES), 0)
    for r in range(rows):
        first = doc_lengths[r, 0]
        second = first + doc_lengths[r, 1]
        third = second + doc_lengths[r, 2]
        ends = jnp.where(line == 0, first, jnp.where(line == 1, second, third))
        info[core, r] = jnp.where(line == 3, slots - pad_counts[r], ends)

    peers = jnp.where(z_half == core, rows - 1, rows)
    pl.semaphore_wait(barrier, peers + seq_size - 1 + group - 1)

    def spread(source, target_ref, at, send_sem, recv_sem, local_sem):
        for r in range(rows):
            target = core * rows + r

            @pl.when(target != z)
            def _():
                remote(
                    source.at[r],
                    target_ref.at[at],
                    send_sem.at[r],
                    recv_sem.at[z - z_half * half_blocks],
                    base + z_half,
                    target,
                ).start()

            @pl.when(target == z)
            def _():
                pltpu.make_async_copy(source.at[r], target_ref.at[at], local_sem).start()

    def spread_done(source, target_ref, at, send_sem, recv_sem):
        for r in range(rows):
            target = core * rows + r

            @pl.when(target != z)
            def _():
                remote(
                    source.at[r],
                    target_ref.at[at],
                    send_sem.at[r],
                    recv_sem.at[z - z_half * half_blocks],
                    base + z_half,
                    target,
                ).wait_send()

    def arrived(source, target_ref, at, block, send_sem, recv_sem, local_sem):
        j = block - core * half_blocks

        @pl.when(block != z)
        def _():
            remote(
                source.at[0],
                target_ref.at[at],
                send_sem.at[0],
                recv_sem.at[j],
                base + z_half,
                block,
            ).wait_recv()

        @pl.when(block == z)
        def _():
            pltpu.make_async_copy(source.at[0], target_ref.at[at], local_sem).wait()

    info_copy = remote(info.at[core], info.at[core], info_sem.at[0], info_sem.at[1], partner, z)
    info_copy.start()
    spread(tokens, row, rows_of(z), tok_send, tok_recv, in_sem.at[0])
    for copy in out_copies:
        copy.start()

    def start_inner(f, carry):
        inner_copy(f).start()
        outer_copy(f).start()
        return carry

    lax.fori_loop(0, chunks, start_inner, 0)

    info_copy.wait_send()
    remote(info.at[far], info.at[far], info_sem.at[0], info_sem.at[1], partner, z).wait_recv()
    for copy in qkv_copies:
        copy.wait()

    lane = lax.broadcasted_iota(jnp.int32, (slots, LANES), 1)
    slot = lax.broadcasted_iota(jnp.int32, (slots, LANES), 0)
    ends = info[z_half, z - z_half * rows]
    doc = (slot >= ends[0:1]).astype(jnp.int32)
    for i in range(1, 4):
        doc = doc + (slot >= ends[i : i + 1]).astype(jnp.int32)
    doc_query = jnp.where(doc == lane, BIG, 0.0).astype(BF16)
    doc_key = jnp.where((doc != lane) & (lane < 5), -1.0, 0.0).astype(BF16)
    ones = jnp.ones((slots, LANES), BF16)

    def pass_on(block):
        j = block - core * half_blocks
        at = rows_of(block)
        return remote(row.at[at], row.at[at], pass_send.at[j], pass_recv.at[j], partner, z)

    def project(step, carry):
        near = step < half_blocks
        within = lax.rem(z - z_half * half_blocks + step, half_blocks)
        other = step - half_blocks
        beyond = jnp.where(z_half == 0, half_blocks + other, half_blocks - 1 - other)
        block = jnp.where(near, z_half * half_blocks + within, beyond)
        block_half = block // half_blocks
        at = rows_of(block)

        @pl.when(block_half == core)
        def _():
            arrived(tokens, row, at, block, tok_send, tok_recv, in_sem.at[0])
            pass_on(block).start()

        @pl.when(block_half != core)
        def _():
            j = block - far * half_blocks
            remote(
                row.at[at], row.at[at], pass_send.at[j], pass_recv.at[j], partner, z
            ).wait_recv()

        x = row[at, :]
        q = (dot(x, m_qkv[:, 0:side]) + bias_query[:, mine]) * score_scale
        k = dot(x, m_qkv[:, side : 2 * side])
        v = dot(x, m_qkv[:, 2 * side : 3 * side]) + bias_value[:, mine]
        for p in range(pairs):
            cut = slice(p * LANES, (p + 1) * LANES)
            qs[p, at, :] = q[:, cut].astype(BF16)
            ks[p, at, :] = k[:, cut].astype(BF16)
            vs[p, at, :] = v[:, cut].astype(BF16)
        return carry

    lax.fori_loop(0, group, project, 0)
    spread_done(tokens, row, rows_of(z), tok_send, tok_recv)

    cot_at = pl.ds(pl.multiple_of((z - z_half * half_blocks) * span, span), span)
    spread(cotangent, cot, cot_at, cot_send, cot_recv, in_sem.at[1])

    def pass_wait(j, carry):
        pass_on(core * half_blocks + j).wait_send()
        return carry

    lax.fori_loop(0, half_blocks, pass_wait, 0)

    lane_row = lax.broadcasted_iota(jnp.int32, (1, LANES), 1)
    head_mask = [
        (lane_row < head_width).astype(F32),
        (lane_row >= head_width).astype(F32),
    ]
    low_mask = [mask.astype(BF16) for mask in head_mask]
    near_rows = pl.ds(pl.multiple_of(core * half, half), half)
    far_rows = pl.ds(pl.multiple_of(far * half, half), half)

    def att_copy(p):
        return remote(
            att.at[p, far_rows], att_far.at[p], att_send.at[p], att_recv.at[p], partner, z
        )

    def attend(p, carry):
        queries, keys = qs[p], jnp.concatenate([ks[p], doc_key], axis=1)
        values = jnp.concatenate([vs[p], ones], axis=1)
        total = None
        shares = None
        for i in range(2):
            left = jnp.concatenate([queries * low_mask[i], doc_query], axis=1)
            scores = dot_nt(left, keys)
            exponent = jnp.exp(scores - jnp.max(scores, axis=-1, keepdims=True)).astype(BF16)
            exps[2 * p + i] = exponent
            both = dot(exponent, values)
            share = 1.0 / both[:, LANES:]
            part = both[:, :LANES] * share * head_mask[i]
            share = share * head_mask[i]
            total = part if total is None else total + part
            shares = share if shares is None else shares + share
        mixed[p] = total
        recip[p] = shares
        att[p] = total.astype(BF16)
        att_copy(p).start()
        return carry

    lax.fori_loop(0, pairs, attend, 0)

    for copy in out_copies:
        copy.wait()

    def att_wait(p, carry):
        att_copy(p).wait()
        return carry

    lax.fori_loop(0, pairs, att_wait, 0)
    left = jnp.concatenate(
        [att[p, near_rows, :] for p in range(pairs)] + [att_far[p] for p in range(pairs)], axis=1
    )
    acc[...] = dot(left, m_out[...])

    norm_steps = half // NORM_ROWS

    def lines_of(step):
        return pl.ds(pl.multiple_of(step * NORM_ROWS, NORM_ROWS), NORM_ROWS)

    def norm_first(step, carry):
        at = lines_of(step)
        near = pl.ds(pl.multiple_of(core * half + step * NORM_ROWS, NORM_ROWS), NORM_ROWS)
        hidden = row[near, :].astype(F32) + acc[at, :] + bias_out[...]
        norm, inv_std = normed(hidden)
        norm_a[at, :] = norm
        inv_a[at, :] = jnp.broadcast_to(inv_std, (NORM_ROWS, LANES))
        middle = norm * gain_attn[...] + beta_attn[...]
        mid[at, :] = middle
        mid_low[at, :] = middle.astype(BF16)
        return carry

    lax.fori_loop(0, norm_steps, norm_first, 0)

    def forward(f, carry):
        inner_copy(f).wait()
        outer_copy(f).wait()
        columns = pl.ds(pl.multiple_of(f * FF_CHUNK, FF_CHUNK), FF_CHUNK)
        inner = dot(mid_low[...], m_inner[f]) + bias_inner[:, columns]
        cdf = 0.5 * (1.0 + lax.erf(inner * 0.7071067811865476))
        slope[f] = cdf + inner * jnp.exp(-0.5 * inner * inner) * 0.3989422804014327
        active = (inner * cdf).astype(BF16)
        more = dot(active, m_outer[f])

        @pl.when(f == 0)
        def _():
            acc[...] = more

        @pl.when(f > 0)
        def _():
            acc[...] += more

        return carry

    lax.fori_loop(0, chunks, forward, 0)

    def cot_wait(j, carry):
        at = pl.ds(pl.multiple_of(j * span, span), span)
        arrived(cotangent, cot, at, core * half_blocks + j, cot_send, cot_recv, in_sem.at[1])
        return carry

    lax.fori_loop(0, half_blocks, cot_wait, 0)
    spread_done(cotangent, cot, cot_at, cot_send, cot_recv)

    live_end = ends[3:4, 0:1]
    zero_sum = jnp.zeros((8, width), F32)

    def norm_last(step, carry):
        beta_sum, outer_sum = carry
        at = lines_of(step)
        hidden = mid[at, :] + acc[at, :] + bias_outer[...]
        norm, inv_std = normed(hidden)
        place = lax.broadcasted_iota(jnp.int32, (NORM_ROWS, 1), 0) + core * half + step * NORM_ROWS
        live = (place < live_end).astype(F32)
        layer_out[at, :] = (live * (norm * gain_final[...] + beta_final[...])).astype(BF16)
        grad_final = live * cot[at, :].astype(F32)
        grad_hidden = norm_back(grad_final * gain_final[...], norm, inv_std)
        grad_h[at, :] = grad_hidden
        grad_low[at, :] = grad_hidden.astype(BF16)
        return beta_sum + fold_rows(grad_final), outer_sum + fold_rows(grad_hidden)

    beta_final_sum, outer_sum = lax.fori_loop(0, norm_steps, norm_last, (zero_sum, zero_sum))
    pool_a[seq, 3:4, :] = jnp.sum(beta_final_sum, axis=0, keepdims=True)
    pool_a[seq, 1:2, :] = jnp.sum(outer_sum, axis=0, keepdims=True)

    def home(source, target_ref, send_sem, recv_sem, local_sem):
        for j in range(half_blocks):
            block = core * half_blocks + j
            src = source.at[j * span : (j + 1) * span]
            line_at = z - z_half * rows

            @pl.when(block != z)
            def _():
                remote(
                    src,
                    target_ref.at[line_at],
                    send_sem.at[j],
                    recv_sem.at[line_at],
                    base + z_half,
                    block,
                ).start()

            @pl.when(block == z)
            def _():
                pltpu.make_async_copy(src, target_ref.at[line_at], local_sem).start()

    def home_done(source, target_ref, send_sem, recv_sem, local_sem):
        for j in range(half_blocks):
            block = core * half_blocks + j
            src = source.at[j * span : (j + 1) * span]
            line_at = z - z_half * rows

            @pl.when(block != z)
            def _():
                remote(
                    src,
                    target_ref.at[line_at],
                    send_sem.at[j],
                    recv_sem.at[line_at],
                    base + z_half,
                    block,
                ).wait_send()

            @pl.when(block == z)
            def _():
                pltpu.make_async_copy(src, target_ref.at[line_at], local_sem).wait()

        for r in range(rows):
            target = core * rows + r

            @pl.when(target != z)
            def _():
                remote(
                    source.at[0:span],
                    target_ref.at[r],
                    send_sem.at[0],
                    recv_sem.at[r],
                    base + z_half,
                    target,
                ).wait_recv()

    home(layer_out, layer_home, lay_send, lay_recv, in_sem.at[2])

    def backward(f, carry):
        grad_active = dot_nt(grad_low[...], m_outer[f])
        grad_inner = (grad_active * slope[f]).astype(BF16)
        total = jnp.sum(fold_rows(grad_inner.astype(F32)), axis=0, keepdims=True)
        per_line = width // FF_CHUNK
        for i in range(per_line):

            @pl.when(lax.rem(f, per_line) == i)
            def _():
                for t in range(chunks // per_line):

                    @pl.when(f // per_line == t)
                    def _():
                        pool_a[seq, 4 + t : 5 + t, i * FF_CHUNK : (i + 1) * FF_CHUNK] = total

        more = dot_nt(grad_inner, m_inner[f])

        @pl.when(f == 0)
        def _():
            acc[...] = more

        @pl.when(f > 0)
        def _():
            acc[...] += more

        return carry

    lax.fori_loop(0, chunks, backward, 0)

    def norm_first_back(step, carry):
        beta_sum, out_sum = carry
        at = lines_of(step)
        grad_middle = grad_h[at, :] + acc[at, :]
        grad_hidden = norm_back(grad_middle * gain_attn[...], norm_a[at, :], inv_a[at, 0:1])
        grad_h[at, :] = grad_hidden
        grad_low[at, :] = grad_hidden.astype(BF16)
        return beta_sum + fold_rows(grad_middle), out_sum + fold_rows(grad_hidden)

    beta_attn_sum, out_sum = lax.fori_loop(0, norm_steps, norm_first_back, (zero_sum, zero_sum))
    pool_a[seq, 2:3, :] = jnp.sum(beta_attn_sum, axis=0, keepdims=True)
    pool_a[seq, 0:1, :] = jnp.sum(out_sum, axis=0, keepdims=True)

    def plane_copy(pool, send_sem, recv_sem, step):
        return remote(
            pool.at[seq],
            pool.at[seq],
            send_sem.at[step],
            recv_sem.at[seq],
            lax.rem(seq + step, seq_size),
            z,
        )

    def plane_start(pool, send_sem, recv_sem):
        def go(step, carry):
            plane_copy(pool, send_sem, recv_sem, step).start()
            return carry

        lax.fori_loop(1, seq_size, go, 0)

    def plane_wait(pool, send_sem, recv_sem):
        def go(step, carry):
            source = lax.rem(seq + step, seq_size)
            plane_copy(pool, send_sem, recv_sem, step).wait_send()
            remote(
                pool.at[source],
                pool.at[source],
                send_sem.at[step],
                recv_sem.at[source],
                source,
                z,
            ).wait_recv()
            return carry

        lax.fori_loop(1, seq_size, go, 0)

    def column_copy(pool, send_sem, recv_sem, step):
        return remote(
            pool.at[z],
            pool.at[z],
            send_sem.at[step],
            recv_sem.at[z],
            seq,
            lax.rem(z + step, group),
        )

    def column_start(pool, send_sem, recv_sem):
        def go(step, carry):
            column_copy(pool, send_sem, recv_sem, step).start()
            return carry

        lax.fori_loop(1, group, go, 0)

    def column_wait(pool, send_sem, recv_sem):
        def go(step, carry):
            source = lax.rem(z + step, group)
            column_copy(pool, send_sem, recv_sem, step).wait_send()
            remote(
                pool.at[source],
                pool.at[source],
                send_sem.at[step],
                recv_sem.at[source],
                seq,
                source,
            ).wait_recv()
            return carry

        lax.fori_loop(1, group, go, 0)

    plane_start(pool_a, pa_send, pa_recv)

    lines = dot_nt(grad_low[...], m_out[...])
    for p in range(pairs):
        grad_att[p, near_rows, :] = lines[:, p * LANES : (p + 1) * LANES].astype(BF16)
        grad_far[p] = lines[:, side + p * LANES : side + (p + 1) * LANES].astype(BF16)

    def gat_copy(p):
        return remote(
            grad_far.at[p], grad_att.at[p, near_rows], gat_send.at[p], gat_recv.at[p], partner, z
        )

    def gat_start(p, carry):
        gat_copy(p).start()
        return carry

    lax.fori_loop(0, pairs, gat_start, 0)

    def attend_back(p, carry):
        gat_copy(p).wait_send()
        remote(
            grad_far.at[p], grad_att.at[p, far_rows], gat_send.at[p], gat_recv.at[p], partner, z
        ).wait_recv()
        queries, keys = qs[p], ks[p]
        values = jnp.concatenate([vs[p], ones], axis=1)
        share = recip[p]
        scaled = (grad_att[p].astype(F32) * share).astype(BF16)
        product = scaled.astype(F32) * mixed[p]
        dq = dk = dv = None
        for i in range(2):
            delta = jnp.sum(product * head_mask[i], axis=-1, keepdims=True)
            high = delta.astype(BF16).astype(F32)
            extra = jnp.where(lane == 0, -high, jnp.where(lane == 1, high - delta, 0.0))
            grads = scaled * low_mask[i]
            left = jnp.concatenate([grads, extra.astype(BF16)], axis=1)
            exponent = exps[2 * p + i]
            grad_scores = (exponent.astype(F32) * dot_nt(left, values)).astype(BF16)
            dq_part = dot(grad_scores, keys * low_mask[i])
            dk_part = dot_tn(grad_scores, queries * low_mask[i])
            dv_part = dot_tn(exponent, grads)
            dq = dq_part if dq is None else dq + dq_part
            dk = dk_part if dk is None else dk + dk_part
            dv = dv_part if dv is None else dv + dv_part
        dq = (dq * score_scale).astype(BF16)
        dv = dv.astype(BF16)
        for i, block in enumerate((dq, dk.astype(BF16), dv)):
            at = pl.ds(pl.multiple_of(i * side + p * LANES, LANES), LANES)
            grad_qkv[:, at] = block
        for t in range(pairs):

            @pl.when(p == t)
            def _():
                pool_b[seq, t : t + 1, :] = jnp.sum(
                    fold_rows(dq.astype(F32)), axis=0, keepdims=True
                )
                pool_b[seq, pairs + t : pairs + t + 1, :] = jnp.sum(
                    fold_rows(dv.astype(F32)), axis=0, keepdims=True
                )

        return carry

    lax.fori_loop(0, pairs, attend_back, 0)
    plane_start(pool_b, pb_send, pb_recv)

    plane_wait(pool_a, pa_send, pa_recv)
    total = pool_a[0]
    for s in range(1, seq_size):
        total = total + pool_a[s]
    z_a[z] = total
    column_start(z_a, za_send, za_recv)

    part_out[...] = dot_nt(grad_qkv[far_rows, :], m_qkv[...]).astype(BF16)
    part_copy = remote(part_out, part_in, part_sem.at[0], part_sem.at[1], partner, z)
    part_copy.start()
    acc[...] = dot_nt(grad_qkv[near_rows, :], m_qkv[...])
    part_copy.wait()

    def finish(step, carry):
        at = lines_of(step)
        total = grad_h[at, :] + acc[at, :] + part_in[at, :].astype(F32)
        grad_out[at, :] = total.astype(BF16)
        return carry

    lax.fori_loop(0, norm_steps, finish, 0)
    home(grad_out, grad_home, grad_send, grad_recv, in_sem.at[3])

    plane_wait(pool_b, pb_send, pb_recv)
    for i in range(2):
        total = pool_b[i]
        for s in range(2 + i, seq_size, 2):
            total = total + pool_b[s]
        z_b[z, i] = total
    column_start(z_b, zb_send, zb_recv)

    column_wait(z_a, za_send, za_recv)
    total = z_a[0]
    for s in range(1, group):
        total = total + z_a[s]
    sums_a[...] = total

    column_wait(z_b, zb_send, zb_recv)
    total = z_b[0]
    for s in range(1, group):
        total = total + z_b[s]
    sums_b[...] = total

    home_done(layer_out, layer_home, lay_send, lay_recv, in_sem.at[2])
    home_done(grad_out, grad_home, grad_send, grad_recv, in_sem.at[3])


def per_device(
    seq_size,
    group,
    tokens,
    doc_lengths,
    pad_counts,
    w_query,
    w_key,
    w_value,
    w_out,
    w_inner,
    w_outer,
    bias_query,
    bias_value,
    bias_out,
    bias_inner,
    bias_outer,
    gain_attn,
    beta_attn,
    gain_final,
    beta_final,
    cotangent,
):
    rows, span, width = tokens.shape
    hidden = w_inner.shape[1]
    slots = span * group
    half = slots // 2
    half_blocks = group // 2
    side = width // 2
    pairs = side // LANES
    chunks = hidden // FF_CHUNK
    if rows * 2 != group or pairs * 2 != 8 or hidden != 4 * width:
        raise ValueError("unsupported sizes")

    any_space = pl.BlockSpec(memory_space=pl.ANY)
    vmem = pl.BlockSpec(memory_space=pltpu.VMEM)
    smem = pl.BlockSpec(memory_space=pltpu.SMEM)
    dma = pltpu.SemaphoreType.DMA
    scratch = [
        pltpu.VMEM((width, 3 * side), BF16),
        pltpu.VMEM((width, width), BF16),
        pltpu.VMEM((chunks, width, FF_CHUNK), BF16),
        pltpu.VMEM((chunks, FF_CHUNK, width), BF16),
        pltpu.VMEM((slots, width), BF16),
        pltpu.VMEM((half, width), BF16),
        pltpu.VMEM((2, rows, 8, LANES), jnp.int32),
        pltpu.VMEM((pairs, slots, LANES), BF16),
        pltpu.VMEM((pairs, slots, LANES), BF16),
        pltpu.VMEM((pairs, slots, LANES), BF16),
        pltpu.VMEM((2 * pairs, slots, slots), BF16),
        pltpu.VMEM((pairs, slots, LANES), F32),
        pltpu.VMEM((pairs, slots, LANES), F32),
        pltpu.VMEM((pairs, slots, LANES), BF16),
        pltpu.VMEM((pairs, half, LANES), BF16),
        pltpu.VMEM((half, width), F32),
        pltpu.VMEM((half, LANES), F32),
        pltpu.VMEM((half, width), F32),
        pltpu.VMEM((half, width), BF16),
        pltpu.VMEM((half, width), F32),
        pltpu.VMEM((chunks, half, FF_CHUNK), F32),
        pltpu.VMEM((half, width), F32),
        pltpu.VMEM((half, width), BF16),
        pltpu.VMEM((pairs, slots, LANES), BF16),
        pltpu.VMEM((pairs, half, LANES), BF16),
        pltpu.VMEM((slots, 3 * side), BF16),
        pltpu.VMEM((half, width), BF16),
        pltpu.VMEM((half, width), BF16),
        pltpu.VMEM((half, width), BF16),
        pltpu.VMEM((half, width), BF16),
        pltpu.VMEM((seq_size, 8, width), F32),
        pltpu.VMEM((group, 8, width), F32),
        pltpu.VMEM((seq_size, 8, LANES), F32),
        pltpu.VMEM((group, 2, 8, LANES), F32),
        dma((5 + 2 * chunks,)),
        dma((4,)),
        dma((rows,)),
        dma((half_blocks,)),
        dma((half_blocks,)),
        dma((half_blocks,)),
        dma((2,)),
        dma((rows,)),
        dma((half_blocks,)),
        dma((pairs,)),
        dma((pairs,)),
        dma((pairs,)),
        dma((pairs,)),
        dma((half_blocks,)),
        dma((rows,)),
        dma((2,)),
        dma((half_blocks,)),
        dma((rows,)),
        dma((seq_size,)),
        dma((seq_size,)),
        dma((group,)),
        dma((group,)),
        dma((seq_size,)),
        dma((seq_size,)),
        dma((group,)),
        dma((group,)),
    ]
    vectors = (
        bias_query,
        bias_value,
        bias_out,
        bias_inner,
        bias_outer,
        gain_attn,
        beta_attn,
        gain_final,
        beta_final,
    )
    layer_home, grad_home, sums_a, sums_b = pl.pallas_call(
        functools.partial(kernel, seq_size, group),
        out_shape=(
            jax.ShapeDtypeStruct(tokens.shape, BF16),
            jax.ShapeDtypeStruct(tokens.shape, BF16),
            jax.ShapeDtypeStruct((8, width), F32),
            jax.ShapeDtypeStruct((2, 8, LANES), F32),
        ),
        in_specs=[any_space] * 2 + [smem] * 2 + [any_space] * 6 + [vmem] * len(vectors),
        out_specs=(any_space, any_space, vmem, vmem),
        scratch_shapes=scratch,
        compiler_params=pltpu.CompilerParams(
            collective_id=0, has_side_effects=True, vmem_limit_bytes=60 * 2**20
        ),
    )(
        tokens,
        cotangent,
        doc_lengths,
        pad_counts,
        w_query,
        w_key,
        w_value,
        w_out,
        w_inner,
        w_outer,
        *[vector.reshape(1, -1) for vector in vectors],
    )
    grad_bias_query = sums_b[:, :pairs].reshape(width)
    grad_bias_value = sums_b[:, pairs:].reshape(width)
    return (
        layer_home,
        grad_home.astype(F32),
        grad_bias_query,
        grad_bias_value,
        sums_a[0],
        sums_a[4:8].reshape(hidden),
        sums_a[1],
        sums_a[2],
        sums_a[3],
    )


def solution(mesh):
    split = P("seq", "head", None)
    placed = (split, P("seq", None), P("seq")) + (P(),) * 15 + (split,)
    return jax.shard_map(
        functools.partial(per_device, mesh.shape["seq"], mesh.shape["head"]),
        mesh=mesh,
        in_specs=placed,
        out_specs=(split, split) + (P(),) * 7,
        check_vma=False,
    )
```

profile of v0, /device:TPU:0, one launch (start us, length us, event | category | flops | bytes accessed | tf_op | source)
XLA Modules:
  0.0 85.7 jit_solution(18202622649138281551)
XLA Ops:
  0.7 76.8 %shard_map.250 = (bf16[2,128,1024]{2,1,0:T(8,128)(2,1)}, bf16[2,128,1024]{2,1,0:T(8,128)(2,1)}, f32[8,1024]{1,0:T(8,128)}, f32[2,8,128]{2,1,0:T(8,128)}) custom-call(bf16[2,128,1024]{2,1,0:T(8,128)(2,1)} %tokens.1, bf16[2,128,1024]{2,1,0:T(8,128)(2,1)} %cotangent.1, s32[2,3]{1,0:T(2,128)} %doc_lengths.1, s32[2]{0:T(128)} %pad_counts.1, ...), custom_call_target="tpu_custom_call" | custom-call | tf_op jit(solution)/shard_map/pallas_call | solution.py:870
  77.4 1.4 %fusion.1 = (f32[2,4,128]{2,1,0:T(4,128)}, f32[2,4,128]{2,1,0:T(4,128)}) fusion(f32[2,8,128]{2,1,0:T(8,128)} %get-tuple-element.15), kind=kLoop, calls=%fused_computation.3 | loop fusion | bytes 16384 | tf_op jit(solution)/shard_map/slice | solution.py:898
  78.8 0.8 slice_bitcast_fusion
  79.5 1.6 %fusion = (f32[1,1024]{1,0:T(1,128)}, f32[1,1024]{1,0:T(1,128)}, f32[1,1024]{1,0:T(1,128)}, f32[1,1024]{1,0:T(1,128)}) fusion(f32[8,1024]{1,0:T(8,128)} %get-tuple-element.16), kind=kLoop, calls=%fused_computation.2 | loop fusion | bytes 32768 | tf_op jit(solution)/shard_map/slice | solution.py:908
  81.1 0.6 copy.30
  81.7 2.1 %convert_element_type.3 = f32[2,128,1024]{2,1,0:T(8,128)} convert(bf16[2,128,1024]{2,1,0:T(8,128)(2,1)} %get-tuple-element.14) | non-fusion elementwise | flops 262144 | bytes 1572864 | tf_op jit(solution)/shard_map/convert_element_type | solution.py:901
  83.8 1.9 %copy.32 = bf16[2,128,1024]{2,1,0:T(8,128)(2,1)} copy(bf16[2,128,1024]{2,1,0:T(8,128)(2,1)} %get-tuple-element.32) | data formatting | bytes 1048576
where the time goes:
time: 86.2 us; the launch traced here: 85.7 us
  Pallas kernels  76.8 us (89%)
  local copies, waits for them, and re-layouts  6.16 us (7%)
  other arithmetic  2.12 us (2%)
    pallas_call x1, Pallas kernels, per_device(): pl.pallas_call(functools.partial(kernel, seq_size, group), out_shape=(jax...  76.8 us
    unnamed x3, local copies, waits for them, and re-layouts  3.24 us
    convert_element_type x1, other arithmetic, per_device(): grad_home.astype(F32)  2.12 us

commit v1 on v0

--- a/solution.py
+++ b/solution.py
@@ -12,6 +12,7 @@
 EPS = 1e-06
 BIG = 2.0**30
 FF_CHUNK = 512
+FEATURE_CHUNK = 256
 NORM_ROWS = 32
 MESH = pl.DeviceIdType.MESH
 F32 = jnp.float32
@@ -65,6 +66,23 @@
     w_out,
     w_inner,
     w_outer,
+    in_bias_query,
+    in_bias_value,
+    in_bias_out,
+    in_bias_inner,
+    in_bias_outer,
+    in_gain_attn,
+    in_beta_attn,
+    in_gain_final,
+    in_beta_final,
+    layer_home,
+    grad_home,
+    sums_a,
+    sums_b,
+    m_qkv,
+    m_out,
+    m_inner,
+    m_outer,
     bias_query,
     bias_value,
     bias_out,
@@ -74,14 +92,6 @@
     beta_attn,
     gain_final,
     beta_final,
-    layer_home,
-    grad_home,
-    sums_a,
-    sums_b,
-    m_qkv,
-    m_out,
-    m_inner,
-    m_outer,
     row,
     cot,
     info,
@@ -99,11 +109,15 @@
     mid_low,
     acc,
     slope,
+    raw,
+    active,
+    inner_sum,
     grad_h,
     grad_low,
     grad_att,
     grad_far,
     grad_qkv,
+    part,
     part_out,
     part_in,
     grad_out,
@@ -113,6 +127,7 @@
     pool_b,
     z_b,
     w_sem,
+    vec_sem,
     in_sem,
     tok_send,
     tok_recv,
@@ -127,7 +142,8 @@
     gat_recv,
     lay_send,
     lay_recv,
-    part_sem,
+    part_send,
+    part_recv,
     grad_send,
     grad_recv,
     pa_send,
@@ -147,6 +163,7 @@
     side = width // 2
     pairs = side // LANES
     chunks = m_inner.shape[0]
+    norm_steps = half // NORM_ROWS
     score_scale = head_width**-0.5
 
     seq = lax.axis_index("seq")
@@ -206,6 +223,24 @@
     ]
     for copy in qkv_copies:
         copy.start()
+    vector_copies = [
+        pltpu.make_async_copy(source, target, vec_sem.at[i])
+        for i, (source, target) in enumerate(
+            (
+                (in_bias_query, bias_query),
+                (in_bias_value, bias_value),
+                (in_bias_out, bias_out),
+                (in_bias_inner, bias_inner),
+                (in_bias_outer, bias_outer),
+                (in_gain_attn, gain_attn),
+                (in_beta_attn, beta_attn),
+                (in_gain_final, gain_final),
+                (in_beta_final, beta_final),
+            )
+        )
+    ]
+    for copy in vector_copies:
+        copy.start()
     out_copies = [
         pltpu.make_async_copy(w_out.at[mine], m_out.at[0:side], w_sem.at[3]),
         pltpu.make_async_copy(w_out.at[theirs], m_out.at[side:width], w_sem.at[4]),
@@ -217,7 +252,7 @@
 
     def outer_copy(f):
         lines = pl.ds(pl.multiple_of(f * FF_CHUNK, FF_CHUNK), FF_CHUNK)
-        return pltpu.make_async_copy(w_outer.at[lines], m_outer.at[f], w_sem.at[5 + chunks + f])
+        return pltpu.make_async_copy(w_outer.at[lines], m_outer.at[lines], w_sem.at[5 + chunks + f])
 
     line = lax.broadcasted_iota(jnp.int32, (8, LANES), 0)
     for r in range(rows):
@@ -297,7 +332,7 @@
 
     info_copy.wait_send()
     remote(info.at[far], info.at[far], info_sem.at[0], info_sem.at[1], partner, z).wait_recv()
-    for copy in qkv_copies:
+    for copy in qkv_copies + vector_copies:
         copy.wait()
 
     lane = lax.broadcasted_iota(jnp.int32, (slots, LANES), 1)
@@ -373,44 +408,52 @@
             att.at[p, far_rows], att_far.at[p], att_send.at[p], att_recv.at[p], partner, z
         )
 
-    def attend(p, carry):
-        queries, keys = qs[p], jnp.concatenate([ks[p], doc_key], axis=1)
+    def score(p):
+        keys = jnp.concatenate([ks[p], doc_key], axis=1)
+        for i in range(2):
+            left = jnp.concatenate([qs[p] * low_mask[i], doc_query], axis=1)
+            slope[2 * lax.rem(p, 2) + i] = dot_nt(left, keys)
+
+    def attend(p):
         values = jnp.concatenate([vs[p], ones], axis=1)
         total = None
         shares = None
         for i in range(2):
-            left = jnp.concatenate([queries * low_mask[i], doc_query], axis=1)
-            scores = dot_nt(left, keys)
+            scores = slope[2 * lax.rem(p, 2) + i]
             exponent = jnp.exp(scores - jnp.max(scores, axis=-1, keepdims=True)).astype(BF16)
             exps[2 * p + i] = exponent
             both = dot(exponent, values)
             share = 1.0 / both[:, LANES:]
-            part = both[:, :LANES] * share * head_mask[i]
+            spread_out = both[:, :LANES] * share * head_mask[i]
             share = share * head_mask[i]
-            total = part if total is None else total + part
+            total = spread_out if total is None else total + spread_out
             shares = share if shares is None else shares + share
         mixed[p] = total
         recip[p] = shares
         att[p] = total.astype(BF16)
         att_copy(p).start()
-        return carry
-
-    lax.fori_loop(0, pairs, attend, 0)
+
+    def attend_step(p, carry):
+        score(p + 1)
+        attend(p)
+        return carry
+
+    score(0)
+    lax.fori_loop(0, pairs - 1, attend_step, 0, unroll=True)
+    attend(pairs - 1)
 
     for copy in out_copies:
         copy.wait()
+    left = jnp.concatenate([att[p, near_rows, :] for p in range(pairs)], axis=1)
+    acc[...] = dot(left, m_out[0:side, :])
 
     def att_wait(p, carry):
         att_copy(p).wait()
         return carry
 
     lax.fori_loop(0, pairs, att_wait, 0)
-    left = jnp.concatenate(
-        [att[p, near_rows, :] for p in range(pairs)] + [att_far[p] for p in range(pairs)], axis=1
-    )
-    acc[...] = dot(left, m_out[...])
-
-    norm_steps = half // NORM_ROWS
+    left = jnp.concatenate([att_far[p] for p in range(pairs)], axis=1)
+    acc[...] += dot(left, m_out[side:width, :])
 
     def lines_of(step):
         return pl.ds(pl.multiple_of(step * NORM_ROWS, NORM_ROWS), NORM_ROWS)
@@ -427,29 +470,38 @@
         mid_low[at, :] = middle.astype(BF16)
         return carry
 
-    lax.fori_loop(0, norm_steps, norm_first, 0)
-
-    def forward(f, carry):
+    lax.fori_loop(0, norm_steps, norm_first, 0, unroll=True)
+
+    def weights_wait(f, carry):
         inner_copy(f).wait()
         outer_copy(f).wait()
-        columns = pl.ds(pl.multiple_of(f * FF_CHUNK, FF_CHUNK), FF_CHUNK)
-        inner = dot(mid_low[...], m_inner[f]) + bias_inner[:, columns]
+        return carry
+
+    lax.fori_loop(0, chunks, weights_wait, 0)
+
+    def columns_of(f):
+        return pl.ds(pl.multiple_of(f * FF_CHUNK, FF_CHUNK), FF_CHUNK)
+
+    def slope_at(f):
+        return f // 2, pl.ds(pl.multiple_of(lax.rem(f, 2) * half, half), half)
+
+    def activate(f):
+        inner = raw[lax.rem(f, 2)] + bias_inner[:, columns_of(f)]
         cdf = 0.5 * (1.0 + lax.erf(inner * 0.7071067811865476))
-        slope[f] = cdf + inner * jnp.exp(-0.5 * inner * inner) * 0.3989422804014327
-        active = (inner * cdf).astype(BF16)
-        more = dot(active, m_outer[f])
-
-        @pl.when(f == 0)
-        def _():
-            acc[...] = more
-
-        @pl.when(f > 0)
-        def _():
-            acc[...] += more
-
-        return carry
-
-    lax.fori_loop(0, chunks, forward, 0)
+        which, lines = slope_at(f)
+        slope[which, lines, :] = cdf + inner * jnp.exp(-0.5 * inner * inner) * 0.3989422804014327
+        active[:, columns_of(f)] = (inner * cdf).astype(BF16)
+
+    def forward(f, carry):
+        raw[lax.rem(f + 1, 2)] = dot(mid_low[...], m_inner[f + 1])
+        activate(f)
+        return carry
+
+    raw[0] = dot(mid_low[...], m_inner[0])
+    lax.fori_loop(0, chunks - 1, forward, 0, unroll=True)
+    activate(chunks - 1)
+    for n in range(0, width, FEATURE_CHUNK):
+        acc[:, n : n + FEATURE_CHUNK] = dot(active[...], m_outer[:, n : n + FEATURE_CHUNK])
 
     def cot_wait(j, carry):
         at = pl.ds(pl.multiple_of(j * span, span), span)
@@ -476,30 +528,31 @@
         grad_low[at, :] = grad_hidden.astype(BF16)
         return beta_sum + fold_rows(grad_final), outer_sum + fold_rows(grad_hidden)
 
-    beta_final_sum, outer_sum = lax.fori_loop(0, norm_steps, norm_last, (zero_sum, zero_sum))
+    beta_final_sum, outer_sum = lax.fori_loop(
+        0, norm_steps, norm_last, (zero_sum, zero_sum), unroll=True
+    )
     pool_a[seq, 3:4, :] = jnp.sum(beta_final_sum, axis=0, keepdims=True)
     pool_a[seq, 1:2, :] = jnp.sum(outer_sum, axis=0, keepdims=True)
 
-    def home(source, target_ref, send_sem, recv_sem, local_sem):
-        for j in range(half_blocks):
-            block = core * half_blocks + j
-            src = source.at[j * span : (j + 1) * span]
-            line_at = z - z_half * rows
-
-            @pl.when(block != z)
-            def _():
-                remote(
-                    src,
-                    target_ref.at[line_at],
-                    send_sem.at[j],
-                    recv_sem.at[line_at],
-                    base + z_half,
-                    block,
-                ).start()
-
-            @pl.when(block == z)
-            def _():
-                pltpu.make_async_copy(src, target_ref.at[line_at], local_sem).start()
+    def home_block(block, source, target_ref, send_sem, recv_sem, local_sem):
+        j = block - core * half_blocks
+        src = source.at[pl.ds(pl.multiple_of(j * span, span), span)]
+        line_at = z - z_half * rows
+
+        @pl.when(block != z)
+        def _():
+            remote(
+                src,
+                target_ref.at[line_at],
+                send_sem.at[j],
+                recv_sem.at[line_at],
+                base + z_half,
+                block,
+            ).start()
+
+        @pl.when(block == z)
+        def _():
+            pltpu.make_async_copy(src, target_ref.at[line_at], local_sem).start()
 
     def home_done(source, target_ref, send_sem, recv_sem, local_sem):
         for j in range(half_blocks):
@@ -536,36 +589,35 @@
                     target,
                 ).wait_recv()
 
-    home(layer_out, layer_home, lay_send, lay_recv, in_sem.at[2])
+    for j in range(half_blocks):
+        home_block(
+            core * half_blocks + j, layer_out, layer_home, lay_send, lay_recv, in_sem.at[2]
+        )
 
     def backward(f, carry):
-        grad_active = dot_nt(grad_low[...], m_outer[f])
-        grad_inner = (grad_active * slope[f]).astype(BF16)
-        total = jnp.sum(fold_rows(grad_inner.astype(F32)), axis=0, keepdims=True)
-        per_line = width // FF_CHUNK
-        for i in range(per_line):
-
-            @pl.when(lax.rem(f, per_line) == i)
-            def _():
-                for t in range(chunks // per_line):
-
-                    @pl.when(f // per_line == t)
-                    def _():
-                        pool_a[seq, 4 + t : 5 + t, i * FF_CHUNK : (i + 1) * FF_CHUNK] = total
-
-        more = dot_nt(grad_inner, m_inner[f])
-
-        @pl.when(f == 0)
-        def _():
-            acc[...] = more
-
-        @pl.when(f > 0)
-        def _():
-            acc[...] += more
-
-        return carry
-
-    lax.fori_loop(0, chunks, backward, 0)
+        which, lines = slope_at(f)
+        grad_active = dot_nt(grad_low[...], m_outer[columns_of(f), :])
+        grad_inner = (grad_active * slope[which, lines, :]).astype(BF16)
+        active[:, columns_of(f)] = grad_inner
+        inner_sum[f] = fold_rows(grad_inner.astype(F32))
+        return carry
+
+    lax.fori_loop(0, chunks, backward, 0, unroll=True)
+    for n in range(0, width, FEATURE_CHUNK):
+        total = None
+        for f in range(chunks):
+            term = dot_nt(
+                active[:, f * FF_CHUNK : (f + 1) * FF_CHUNK], m_inner[f, n : n + FEATURE_CHUNK, :]
+            )
+            total = term if total is None else total + term
+        acc[:, n : n + FEATURE_CHUNK] = total
+    per_line = width // FF_CHUNK
+    for f in range(chunks):
+        line_at = 4 + f // per_line
+        column = f % per_line * FF_CHUNK
+        pool_a[seq, line_at : line_at + 1, column : column + FF_CHUNK] = jnp.sum(
+            inner_sum[f], axis=0, keepdims=True
+        )
 
     def norm_first_back(step, carry):
         beta_sum, out_sum = carry
@@ -576,7 +628,9 @@
         grad_low[at, :] = grad_hidden.astype(BF16)
         return beta_sum + fold_rows(grad_middle), out_sum + fold_rows(grad_hidden)
 
-    beta_attn_sum, out_sum = lax.fori_loop(0, norm_steps, norm_first_back, (zero_sum, zero_sum))
+    beta_attn_sum, out_sum = lax.fori_loop(
+        0, norm_steps, norm_first_back, (zero_sum, zero_sum), unroll=True
+    )
     pool_a[seq, 2:3, :] = jnp.sum(beta_attn_sum, axis=0, keepdims=True)
     pool_a[seq, 0:1, :] = jnp.sum(out_sum, axis=0, keepdims=True)
 
@@ -648,34 +702,39 @@
 
     plane_start(pool_a, pa_send, pa_recv)
 
-    lines = dot_nt(grad_low[...], m_out[...])
-    for p in range(pairs):
-        grad_att[p, near_rows, :] = lines[:, p * LANES : (p + 1) * LANES].astype(BF16)
-        grad_far[p] = lines[:, side + p * LANES : side + (p + 1) * LANES].astype(BF16)
-
     def gat_copy(p):
         return remote(
             grad_far.at[p], grad_att.at[p, near_rows], gat_send.at[p], gat_recv.at[p], partner, z
         )
 
-    def gat_start(p, carry):
+    lines = dot_nt(grad_low[...], m_out[side:width, :])
+    for p in range(pairs):
+        grad_far[p] = lines[:, p * LANES : (p + 1) * LANES].astype(BF16)
         gat_copy(p).start()
-        return carry
-
-    lax.fori_loop(0, pairs, gat_start, 0)
-
-    def attend_back(p, carry):
+    lines = dot_nt(grad_low[...], m_out[0:side, :])
+    for p in range(pairs):
+        grad_att[p, near_rows, :] = lines[:, p * LANES : (p + 1) * LANES].astype(BF16)
+
+    def gat_wait(p, carry):
         gat_copy(p).wait_send()
         remote(
             grad_far.at[p], grad_att.at[p, far_rows], gat_send.at[p], gat_recv.at[p], partner, z
         ).wait_recv()
-        queries, keys = qs[p], ks[p]
+        return carry
+
+    lax.fori_loop(0, pairs, gat_wait, 0)
+
+    def attend_back(p, carry):
+        keys = ks[p]
+        turned = qs[p].T
         values = jnp.concatenate([vs[p], ones], axis=1)
-        share = recip[p]
-        scaled = (grad_att[p].astype(F32) * share).astype(BF16)
+        scaled = (grad_att[p].astype(F32) * recip[p]).astype(BF16)
         product = scaled.astype(F32) * mixed[p]
-        dq = dk = dv = None
+        dq = None
+        dk = []
+        dv = []
         for i in range(2):
+            cut = slice(i * head_width, (i + 1) * head_width)
             delta = jnp.sum(product * head_mask[i], axis=-1, keepdims=True)
             high = delta.astype(BF16).astype(F32)
             extra = jnp.where(lane == 0, -high, jnp.where(lane == 1, high - delta, 0.0))
@@ -683,31 +742,23 @@
             left = jnp.concatenate([grads, extra.astype(BF16)], axis=1)
             exponent = exps[2 * p + i]
             grad_scores = (exponent.astype(F32) * dot_nt(left, values)).astype(BF16)
-            dq_part = dot(grad_scores, keys * low_mask[i])
-            dk_part = dot_tn(grad_scores, queries * low_mask[i])
-            dv_part = dot_tn(exponent, grads)
-            dq = dq_part if dq is None else dq + dq_part
-            dk = dk_part if dk is None else dk + dk_part
-            dv = dv_part if dv is None else dv + dv_part
+            term = dot(grad_scores, keys * low_mask[i])
+            dq = term if dq is None else dq + term
+            dk.append(dot(turned[cut], grad_scores))
+            dv.append(dot(grads.T[cut], exponent))
         dq = (dq * score_scale).astype(BF16)
-        dv = dv.astype(BF16)
-        for i, block in enumerate((dq, dk.astype(BF16), dv)):
+        dk = jnp.concatenate(dk, axis=0).astype(BF16).T
+        dv = jnp.concatenate(dv, axis=0).astype(BF16).T
+        for i, block in enumerate((dq, dk, dv)):
             at = pl.ds(pl.multiple_of(i * side + p * LANES, LANES), LANES)
             grad_qkv[:, at] = block
-        for t in range(pairs):
-
-            @pl.when(p == t)
-            def _():
-                pool_b[seq, t : t + 1, :] = jnp.sum(
-                    fold_rows(dq.astype(F32)), axis=0, keepdims=True
-                )
-                pool_b[seq, pairs + t : pairs + t + 1, :] = jnp.sum(
-                    fold_rows(dv.astype(F32)), axis=0, keepdims=True
-                )
-
-        return carry
-
-    lax.fori_loop(0, pairs, attend_back, 0)
+        pool_b[seq, pl.ds(p, 1), :] = jnp.sum(fold_rows(dq.astype(F32)), axis=0, keepdims=True)
+        pool_b[seq, pl.ds(pairs + p, 1), :] = jnp.sum(
+            fold_rows(dv.astype(F32)), axis=0, keepdims=True
+        )
+        return carry
+
+    lax.fori_loop(0, pairs, attend_back, 0, unroll=True)
     plane_start(pool_b, pb_send, pb_recv)
 
     plane_wait(pool_a, pa_send, pa_recv)
@@ -717,20 +768,61 @@
     z_a[z] = total
     column_start(z_a, za_send, za_recv)
 
-    part_out[...] = dot_nt(grad_qkv[far_rows, :], m_qkv[...]).astype(BF16)
-    part_copy = remote(part_out, part_in, part_sem.at[0], part_sem.at[1], partner, z)
-    part_copy.start()
-    acc[...] = dot_nt(grad_qkv[near_rows, :], m_qkv[...])
-    part_copy.wait()
-
-    def finish(step, carry):
-        at = lines_of(step)
-        total = grad_h[at, :] + acc[at, :] + part_in[at, :].astype(F32)
-        grad_out[at, :] = total.astype(BF16)
-        return carry
-
-    lax.fori_loop(0, norm_steps, finish, 0)
-    home(grad_out, grad_home, grad_send, grad_recv, in_sem.at[3])
+    def block_at(step):
+        first = step < half_blocks
+        near = jnp.where(first, 1 - z_half, z_half)
+        return near * half_blocks + lax.rem(step, half_blocks)
+
+    def slice_of(block):
+        start = (block - block // half_blocks * half_blocks) * span
+        return pl.ds(pl.multiple_of(start, span), span)
+
+    def part_copy(block):
+        j = block - block // half_blocks * half_blocks
+        at = slice_of(block)
+        return remote(
+            part_out.at[at], part_in.at[at], part_send.at[j], part_recv.at[j], partner, z
+        )
+
+    def finish(step):
+        block = block_at(step)
+
+        @pl.when(block // half_blocks == core)
+        def _():
+            at = slice_of(block)
+            part_copy(block).wait_recv()
+            total = grad_h[at, :] + part[lax.rem(step, 2)] + part_in[at, :].astype(F32)
+            grad_out[at, :] = total.astype(BF16)
+            home_block(block, grad_out, grad_home, grad_send, grad_recv, in_sem.at[3])
+
+    def token_grad(step, carry):
+        block = block_at(step)
+        term = dot_nt(grad_qkv[rows_of(block), :], m_qkv[...])
+        mine_now = block // half_blocks == core
+
+        @pl.when(mine_now)
+        def _():
+            part[lax.rem(step, 2)] = term
+
+        @pl.when(jnp.logical_not(mine_now))
+        def _():
+            part_out[slice_of(block), :] = term.astype(BF16)
+            part_copy(block).start()
+
+        @pl.when(step > 0)
+        def _():
+            finish(step - 1)
+
+        return carry
+
+    lax.fori_loop(0, group, token_grad, 0)
+    finish(group - 1)
+
+    def part_wait(j, carry):
+        part_copy(far * half_blocks + j).wait_send()
+        return carry
+
+    lax.fori_loop(0, half_blocks, part_wait, 0)
 
     plane_wait(pool_b, pb_send, pb_recv)
     for i in range(2):
@@ -754,6 +846,59 @@
 
     home_done(layer_out, layer_home, lay_send, lay_recv, in_sem.at[2])
     home_done(grad_out, grad_home, grad_send, grad_recv, in_sem.at[3])
+
+
+def finish_kernel(
+    layer,
+    grad,
+    sums_a,
+    sums_b,
+    layer_out,
+    input_grad,
+    grad_bias_query,
+    grad_bias_value,
+    grad_bias_out,
+    grad_bias_inner,
+    grad_bias_outer,
+    grad_beta_attn,
+    grad_beta_final,
+    wide,
+    lines,
+    inner_line,
+    sems,
+):
+    rows = layer.shape[0]
+    width = layer.shape[2]
+    copies = [pltpu.make_async_copy(layer, layer_out, sems.at[0])]
+    copies[0].start()
+    for r in range(rows):
+        wide[r] = grad[r].astype(F32)
+        copies.append(pltpu.make_async_copy(wide.at[r], input_grad.at[r], sems.at[1 + r]))
+        copies[-1].start()
+    pairs = sums_b.shape[1] // 2
+    for i in range(2):
+        for p in range(pairs):
+            column = (i * pairs + p) * LANES
+            lines[0, :, column : column + LANES] = sums_b[i, p : p + 1, :]
+            lines[1, :, column : column + LANES] = sums_b[i, pairs + p : pairs + p + 1, :]
+    for i in range(4):
+        lines[2 + i] = sums_a[i : i + 1, :]
+        inner_line[:, i * width : (i + 1) * width] = sums_a[4 + i : 5 + i, :]
+    targets = (
+        grad_bias_query,
+        grad_bias_value,
+        grad_bias_out,
+        grad_bias_outer,
+        grad_beta_attn,
+        grad_beta_final,
+    )
+    for i, target in enumerate(targets):
+        copies.append(pltpu.make_async_copy(lines.at[i], target, sems.at[1 + rows + i]))
+        copies[-1].start()
+    copies.append(pltpu.make_async_copy(inner_line, grad_bias_inner, sems.at[7 + rows]))
+    copies[-1].start()
+    for copy in copies:
+        copy.wait()
 
 
 def per_device(
@@ -787,7 +932,7 @@
     side = width // 2
     pairs = side // LANES
     chunks = hidden // FF_CHUNK
-    if rows * 2 != group or pairs * 2 != 8 or hidden != 4 * width:
+    if rows * 2 != group or pairs != 4 or hidden != 4 * width or slots != FF_CHUNK:
         raise ValueError("unsupported sizes")
 
     any_space = pl.BlockSpec(memory_space=pl.ANY)
@@ -798,7 +943,16 @@
         pltpu.VMEM((width, 3 * side), BF16),
         pltpu.VMEM((width, width), BF16),
         pltpu.VMEM((chunks, width, FF_CHUNK), BF16),
-        pltpu.VMEM((chunks, FF_CHUNK, width), BF16),
+        pltpu.VMEM((hidden, width), BF16),
+        pltpu.VMEM((1, width), F32),
+        pltpu.VMEM((1, width), F32),
+        pltpu.VMEM((1, width), F32),
+        pltpu.VMEM((1, hidden), F32),
+        pltpu.VMEM((1, width), F32),
+        pltpu.VMEM((1, width), F32),
+        pltpu.VMEM((1, width), F32),
+        pltpu.VMEM((1, width), F32),
+        pltpu.VMEM((1, width), F32),
         pltpu.VMEM((slots, width), BF16),
         pltpu.VMEM((half, width), BF16),
         pltpu.VMEM((2, rows, 8, LANES), jnp.int32),
@@ -815,12 +969,16 @@
         pltpu.VMEM((half, width), F32),
         pltpu.VMEM((half, width), BF16),
         pltpu.VMEM((half, width), F32),
-        pltpu.VMEM((chunks, half, FF_CHUNK), F32),
+        pltpu.VMEM((chunks // 2, slots, slots), F32),
+        pltpu.VMEM((2, half, FF_CHUNK), F32),
+        pltpu.VMEM((half, hidden), BF16),
+        pltpu.VMEM((chunks, 8, FF_CHUNK), F32),
         pltpu.VMEM((half, width), F32),
         pltpu.VMEM((half, width), BF16),
         pltpu.VMEM((pairs, slots, LANES), BF16),
         pltpu.VMEM((pairs, half, LANES), BF16),
         pltpu.VMEM((slots, 3 * side), BF16),
+        pltpu.VMEM((2, span, width), F32),
         pltpu.VMEM((half, width), BF16),
         pltpu.VMEM((half, width), BF16),
         pltpu.VMEM((half, width), BF16),
@@ -830,6 +988,7 @@
         pltpu.VMEM((seq_size, 8, LANES), F32),
         pltpu.VMEM((group, 2, 8, LANES), F32),
         dma((5 + 2 * chunks,)),
+        dma((9,)),
         dma((4,)),
         dma((rows,)),
         dma((half_blocks,)),
@@ -844,7 +1003,8 @@
         dma((pairs,)),
         dma((half_blocks,)),
         dma((rows,)),
-        dma((2,)),
+        dma((half_blocks,)),
+        dma((half_blocks,)),
         dma((half_blocks,)),
         dma((rows,)),
         dma((seq_size,)),
@@ -870,16 +1030,16 @@
     layer_home, grad_home, sums_a, sums_b = pl.pallas_call(
         functools.partial(kernel, seq_size, group),
         out_shape=(
-            jax.ShapeDtypeStruct(tokens.shape, BF16),
-            jax.ShapeDtypeStruct(tokens.shape, BF16),
-            jax.ShapeDtypeStruct((8, width), F32),
-            jax.ShapeDtypeStruct((2, 8, LANES), F32),
+            pltpu.VMEM(tokens.shape, BF16),
+            pltpu.VMEM(tokens.shape, BF16),
+            pltpu.VMEM((8, width), F32),
+            pltpu.VMEM((2, 8, LANES), F32),
         ),
-        in_specs=[any_space] * 2 + [smem] * 2 + [any_space] * 6 + [vmem] * len(vectors),
-        out_specs=(any_space, any_space, vmem, vmem),
+        in_specs=[any_space] * 2 + [smem] * 2 + [any_space] * (6 + len(vectors)),
+        out_specs=(vmem,) * 4,
         scratch_shapes=scratch,
         compiler_params=pltpu.CompilerParams(
-            collective_id=0, has_side_effects=True, vmem_limit_bytes=60 * 2**20
+            collective_id=0, has_side_effects=True, vmem_limit_bytes=58 * 2**20
         ),
     )(
         tokens,
@@ -894,19 +1054,31 @@
         w_outer,
         *[vector.reshape(1, -1) for vector in vectors],
     )
-    grad_bias_query = sums_b[:, :pairs].reshape(width)
-    grad_bias_value = sums_b[:, pairs:].reshape(width)
-    return (
-        layer_home,
-        grad_home.astype(F32),
-        grad_bias_query,
-        grad_bias_value,
-        sums_a[0],
-        sums_a[4:8].reshape(hidden),
-        sums_a[1],
-        sums_a[2],
-        sums_a[3],
-    )
+    line = jax.ShapeDtypeStruct((1, width), F32)
+    results = pl.pallas_call(
+        finish_kernel,
+        out_shape=(
+            jax.ShapeDtypeStruct(tokens.shape, BF16),
+            jax.ShapeDtypeStruct(tokens.shape, F32),
+            line,
+            line,
+            line,
+            jax.ShapeDtypeStruct((1, hidden), F32),
+            line,
+            line,
+            line,
+        ),
+        in_specs=[vmem] * 4,
+        out_specs=(any_space,) * 9,
+        scratch_shapes=[
+            pltpu.VMEM(tokens.shape, F32),
+            pltpu.VMEM((6, 1, width), F32),
+            pltpu.VMEM((1, hidden), F32),
+            dma((8 + rows,)),
+        ],
+        compiler_params=pltpu.CompilerParams(vmem_limit_bytes=32 * 2**20),
+    )(layer_home, grad_home, sums_a, sums_b)
+    return tuple(results[:2]) + tuple(vector.reshape(-1) for vector in results[2:])
 
 
 def solution(mesh):

time: 86.2 us -> 66.3 us (0.77)
  Pallas kernels: 76.8 us -> 65.3 us
  local copies, waits for them, and re-layouts: 6.16 us -> 0 us
  other arithmetic: 2.12 us -> 0 us
    pallas_call x1 -> x2, Pallas kernels: 76.8 us -> 65.3 us  [the longest x1 64 us: per_device(): pl.pallas_call(functools.partial(kernel, seq_size, group), out_shape=(plt...]
    unnamed x3 -> x0, local copies, waits for them, and re-layouts: 3.24 us -> none
    slice x2 -> x0, local copies, waits for them, and re-layouts: 2.92 us -> none  [the longest x1 1.55 us: per_device(): sums_a[3]]
    convert_element_type x1 -> x0, other arithmetic: 2.12 us -> none  [per_device(): grad_home.astype(F32)]
where the time goes in v1:
time: 66.3 us; the launch traced here: 66.1 us
  Pallas kernels  65.3 us (98%)
  between operations  0.82 us (1%)
    pallas_call x1, Pallas kernels, per_device(): pl.pallas_call(functools.partial(kernel, seq_size, group), out_shape=(plt...  64 us

profile of v1, /device:TPU:0, one launch (start us, length us, event | category | flops | bytes accessed | tf_op | source)
XLA Modules:
  0.0 66.1 jit_solution(3953793576852729806)
XLA Ops:
  0.7 64.0 %shard_map.250 = (bf16[2,128,1024]{2,1,0:T(8,128)(2,1)S(1)}, bf16[2,128,1024]{2,1,0:T(8,128)(2,1)S(1)}, f32[8,1024]{1,0:T(8,128)S(1)}, f32[2,8,128]{2,1,0:T(8,128)S(1)}) custom-call(bf16[2,128,1024]{2,1,0:T(8,128)(2,1)} %tokens.1, bf16[2,128,1024]{2,1,0:T(8,128)(2,1)} %cotangent.1, s32[2,3]{1,0:T(2,128)} %doc_lengths.1, s32[2]{0:T(128)} %pad_counts.1, ...), custom_call_target="tpu_custom_call" | custom-call | tf_op jit(solution)/shard_map/pallas_call | solution.py:1030
  64.7 1.2 %shard_map.251 = (bf16[2,128,1024]{2,1,0:T(8,128)(2,1)}, f32[2,128,1024]{2,1,0:T(8,128)}, f32[1,1024]{1,0:T(1,128)}, f32[1,1024]{1,0:T(1,128)}, f32[1,1024]{1,0:...) custom-call(bf16[2,128,1024]{2,1,0:T(8,128)(2,1)S(1)} %get-tuple-element.22.layer, ...), custom_call_target="tpu_custom_call" | custom-call | tf_op jit(solution)/shard_map/pallas_call | solution.py:1058

commit v2 on v1

--- a/solution.py
+++ b/solution.py
@@ -117,11 +117,15 @@
     grad_att,
     grad_far,
     grad_qkv,
+    key_part,
+    value_part,
+    docs,
     part,
     part_out,
     part_in,
     grad_out,
     layer_out,
+    vec_a,
     pool_a,
     z_a,
     pool_b,
@@ -150,6 +154,8 @@
     pa_recv,
     za_send,
     za_recv,
+    ga_send,
+    ga_recv,
     pb_send,
     pb_recv,
     zb_send,
@@ -165,6 +171,8 @@
     chunks = m_inner.shape[0]
     norm_steps = half // NORM_ROWS
     score_scale = head_width**-0.5
+    slices = sums_a.shape[0]
+    slice_width = width // slices
 
     seq = lax.axis_index("seq")
     z = lax.axis_index("head")
@@ -408,39 +416,41 @@
             att.at[p, far_rows], att_far.at[p], att_send.at[p], att_recv.at[p], partner, z
         )
 
-    def score(p):
+    def score(unit):
+        at, p, spot = unit
         keys = jnp.concatenate([ks[p], doc_key], axis=1)
         for i in range(2):
-            left = jnp.concatenate([qs[p] * low_mask[i], doc_query], axis=1)
-            slope[2 * lax.rem(p, 2) + i] = dot_nt(left, keys)
-
-    def attend(p):
+            left = jnp.concatenate([qs[p, at, :] * low_mask[i], docs[at, :]], axis=1)
+            slope[2 * spot + i, 0:half, :] = dot_nt(left, keys)
+
+    def attend(unit):
+        at, p, spot = unit
         values = jnp.concatenate([vs[p], ones], axis=1)
         total = None
         shares = None
         for i in range(2):
-            scores = slope[2 * lax.rem(p, 2) + i]
+            scores = slope[2 * spot + i, 0:half, :]
             exponent = jnp.exp(scores - jnp.max(scores, axis=-1, keepdims=True)).astype(BF16)
-            exps[2 * p + i] = exponent
+            exps[2 * p + i, at, :] = exponent
             both = dot(exponent, values)
             share = 1.0 / both[:, LANES:]
             spread_out = both[:, :LANES] * share * head_mask[i]
             share = share * head_mask[i]
             total = spread_out if total is None else total + spread_out
             shares = share if shares is None else shares + share
-        mixed[p] = total
-        recip[p] = shares
-        att[p] = total.astype(BF16)
-        att_copy(p).start()
-
-    def attend_step(p, carry):
-        score(p + 1)
-        attend(p)
-        return carry
-
-    score(0)
-    lax.fori_loop(0, pairs - 1, attend_step, 0, unroll=True)
-    attend(pairs - 1)
+        mixed[p, at, :] = total
+        recip[p, at, :] = shares
+        att[p, at, :] = total.astype(BF16)
+
+    docs[...] = doc_query
+    units = [(at, p, p % 2) for at in (far_rows, near_rows) for p in range(pairs)]
+    score(units[0])
+    for i, unit in enumerate(units):
+        if i + 1 < len(units):
+            score(units[i + 1])
+        attend(unit)
+        if i < pairs:
+            att_copy(i).start()
 
     for copy in out_copies:
         copy.wait()
@@ -479,27 +489,22 @@
 
     lax.fori_loop(0, chunks, weights_wait, 0)
 
-    def columns_of(f):
-        return pl.ds(pl.multiple_of(f * FF_CHUNK, FF_CHUNK), FF_CHUNK)
-
     def slope_at(f):
-        return f // 2, pl.ds(pl.multiple_of(lax.rem(f, 2) * half, half), half)
+        return f // 2, slice(f % 2 * half, (f % 2 + 1) * half)
 
     def activate(f):
-        inner = raw[lax.rem(f, 2)] + bias_inner[:, columns_of(f)]
+        columns = slice(f * FF_CHUNK, (f + 1) * FF_CHUNK)
+        inner = raw[f % 2] + bias_inner[:, columns]
         cdf = 0.5 * (1.0 + lax.erf(inner * 0.7071067811865476))
         which, lines = slope_at(f)
         slope[which, lines, :] = cdf + inner * jnp.exp(-0.5 * inner * inner) * 0.3989422804014327
-        active[:, columns_of(f)] = (inner * cdf).astype(BF16)
-
-    def forward(f, carry):
-        raw[lax.rem(f + 1, 2)] = dot(mid_low[...], m_inner[f + 1])
+        active[:, columns] = (inner * cdf).astype(BF16)
+
+    raw[0] = dot(mid_low[...], m_inner[0])
+    for f in range(chunks):
+        if f + 1 < chunks:
+            raw[(f + 1) % 2] = dot(mid_low[...], m_inner[f + 1])
         activate(f)
-        return carry
-
-    raw[0] = dot(mid_low[...], m_inner[0])
-    lax.fori_loop(0, chunks - 1, forward, 0, unroll=True)
-    activate(chunks - 1)
     for n in range(0, width, FEATURE_CHUNK):
         acc[:, n : n + FEATURE_CHUNK] = dot(active[...], m_outer[:, n : n + FEATURE_CHUNK])
 
@@ -509,7 +514,6 @@
         return carry
 
     lax.fori_loop(0, half_blocks, cot_wait, 0)
-    spread_done(cotangent, cot, cot_at, cot_send, cot_recv)
 
     live_end = ends[3:4, 0:1]
     zero_sum = jnp.zeros((8, width), F32)
@@ -528,12 +532,6 @@
         grad_low[at, :] = grad_hidden.astype(BF16)
         return beta_sum + fold_rows(grad_final), outer_sum + fold_rows(grad_hidden)
 
-    beta_final_sum, outer_sum = lax.fori_loop(
-        0, norm_steps, norm_last, (zero_sum, zero_sum), unroll=True
-    )
-    pool_a[seq, 3:4, :] = jnp.sum(beta_final_sum, axis=0, keepdims=True)
-    pool_a[seq, 1:2, :] = jnp.sum(outer_sum, axis=0, keepdims=True)
-
     def home_block(block, source, target_ref, send_sem, recv_sem, local_sem):
         j = block - core * half_blocks
         src = source.at[pl.ds(pl.multiple_of(j * span, span), span)]
@@ -589,20 +587,25 @@
                     target,
                 ).wait_recv()
 
+    block_steps = span // NORM_ROWS
+    sums = (zero_sum, zero_sum)
     for j in range(half_blocks):
+        sums = lax.fori_loop(
+            j * block_steps, (j + 1) * block_steps, norm_last, sums, unroll=True
+        )
         home_block(
             core * half_blocks + j, layer_out, layer_home, lay_send, lay_recv, in_sem.at[2]
         )
-
-    def backward(f, carry):
+    vec_a[3:4, :] = jnp.sum(sums[0], axis=0, keepdims=True)
+    vec_a[1:2, :] = jnp.sum(sums[1], axis=0, keepdims=True)
+
+    for f in range(chunks):
         which, lines = slope_at(f)
-        grad_active = dot_nt(grad_low[...], m_outer[columns_of(f), :])
+        columns = slice(f * FF_CHUNK, (f + 1) * FF_CHUNK)
+        grad_active = dot_nt(grad_low[...], m_outer[columns, :])
         grad_inner = (grad_active * slope[which, lines, :]).astype(BF16)
-        active[:, columns_of(f)] = grad_inner
+        active[:, columns] = grad_inner
         inner_sum[f] = fold_rows(grad_inner.astype(F32))
-        return carry
-
-    lax.fori_loop(0, chunks, backward, 0, unroll=True)
     for n in range(0, width, FEATURE_CHUNK):
         total = None
         for f in range(chunks):
@@ -615,7 +618,7 @@
     for f in range(chunks):
         line_at = 4 + f // per_line
         column = f % per_line * FF_CHUNK
-        pool_a[seq, line_at : line_at + 1, column : column + FF_CHUNK] = jnp.sum(
+        vec_a[line_at : line_at + 1, column : column + FF_CHUNK] = jnp.sum(
             inner_sum[f], axis=0, keepdims=True
         )
 
@@ -631,76 +634,73 @@
     beta_attn_sum, out_sum = lax.fori_loop(
         0, norm_steps, norm_first_back, (zero_sum, zero_sum), unroll=True
     )
-    pool_a[seq, 2:3, :] = jnp.sum(beta_attn_sum, axis=0, keepdims=True)
-    pool_a[seq, 0:1, :] = jnp.sum(out_sum, axis=0, keepdims=True)
-
-    def plane_copy(pool, send_sem, recv_sem, step):
-        return remote(
-            pool.at[seq],
-            pool.at[seq],
-            send_sem.at[step],
-            recv_sem.at[seq],
-            lax.rem(seq + step, seq_size),
-            z,
-        )
-
-    def plane_start(pool, send_sem, recv_sem):
+    vec_a[2:3, :] = jnp.sum(beta_attn_sum, axis=0, keepdims=True)
+    vec_a[0:1, :] = jnp.sum(out_sum, axis=0, keepdims=True)
+
+    def all_peers(start, size, here, make, wait):
         def go(step, carry):
-            plane_copy(pool, send_sem, recv_sem, step).start()
+            peer = start + lax.rem(here - start + step, size)
+            send, receive = make(step, peer)
+            if wait:
+                remote(*send).wait_send()
+                remote(*receive).wait_recv()
+            else:
+                remote(*send).start()
             return carry
 
-        lax.fori_loop(1, seq_size, go, 0)
-
-    def plane_wait(pool, send_sem, recv_sem):
-        def go(step, carry):
-            source = lax.rem(seq + step, seq_size)
-            plane_copy(pool, send_sem, recv_sem, step).wait_send()
-            remote(
-                pool.at[source],
-                pool.at[source],
-                send_sem.at[step],
-                recv_sem.at[source],
-                source,
+        lax.fori_loop(1, size, go, 0)
+
+    def plane_a(step, peer):
+        piece = pl.ds(pl.multiple_of(lax.rem(peer, slices) * slice_width, LANES), slice_width)
+        return (
+            (vec_a.at[:, piece], pool_a.at[seq], pa_send.at[step], pa_recv.at[seq], peer, z),
+            (vec_a.at[:, piece], pool_a.at[peer], pa_send.at[step], pa_recv.at[peer], peer, z),
+        )
+
+    def column_a(step, peer):
+        return (
+            (z_a.at[z], z_a.at[z], za_send.at[step], za_recv.at[z], seq, peer),
+            (z_a.at[peer], z_a.at[peer], za_send.at[step], za_recv.at[peer], seq, peer),
+        )
+
+    own_slice = lax.rem(seq, slices)
+
+    def gather_a(step, peer):
+        there = lax.rem(peer, slices)
+        return (
+            (
+                sums_a.at[own_slice],
+                sums_a.at[own_slice],
+                ga_send.at[step],
+                ga_recv.at[own_slice],
+                peer,
                 z,
-            ).wait_recv()
-            return carry
-
-        lax.fori_loop(1, seq_size, go, 0)
-
-    def column_copy(pool, send_sem, recv_sem, step):
-        return remote(
-            pool.at[z],
-            pool.at[z],
-            send_sem.at[step],
-            recv_sem.at[z],
-            seq,
-            lax.rem(z + step, group),
-        )
-
-    def column_start(pool, send_sem, recv_sem):
-        def go(step, carry):
-            column_copy(pool, send_sem, recv_sem, step).start()
-            return carry
-
-        lax.fori_loop(1, group, go, 0)
-
-    def column_wait(pool, send_sem, recv_sem):
-        def go(step, carry):
-            source = lax.rem(z + step, group)
-            column_copy(pool, send_sem, recv_sem, step).wait_send()
-            remote(
-                pool.at[source],
-                pool.at[source],
-                send_sem.at[step],
-                recv_sem.at[source],
-                seq,
-                source,
-            ).wait_recv()
-            return carry
-
-        lax.fori_loop(1, group, go, 0)
-
-    plane_start(pool_a, pa_send, pa_recv)
+            ),
+            (
+                sums_a.at[there], sums_a.at[there], ga_send.at[step], ga_recv.at[there], peer, z
+            ),
+        )
+
+    def column_b(step, peer):
+        return (
+            (z_b.at[z], z_b.at[z], zb_send.at[step], zb_recv.at[z], seq, peer),
+            (z_b.at[peer], z_b.at[peer], zb_send.at[step], zb_recv.at[peer], seq, peer),
+        )
+
+    def plane_b(step, peer):
+        return (
+            (pool_b.at[seq], pool_b.at[seq], pb_send.at[step], pb_recv.at[seq], peer, z),
+            (pool_b.at[peer], pool_b.at[peer], pb_send.at[step], pb_recv.at[peer], peer, z),
+        )
+
+    def total_of(pool, places):
+        total = pool[places[0]]
+        for place in places[1:]:
+            total = total + pool[place]
+        return total
+
+    all_peers(0, seq_size, seq, plane_a, False)
+    pool_a[seq] = vec_a[:, pl.ds(pl.multiple_of(own_slice * slice_width, LANES), slice_width)]
 
     def gat_copy(p):
         return remote(
@@ -722,14 +722,12 @@
         ).wait_recv()
         return carry
 
-    lax.fori_loop(0, pairs, gat_wait, 0)
-
-    def attend_back(p, carry):
+    def attend_back(at, p, first):
         keys = ks[p]
-        turned = qs[p].T
+        turned = qs[p, at, :].T
         values = jnp.concatenate([vs[p], ones], axis=1)
-        scaled = (grad_att[p].astype(F32) * recip[p]).astype(BF16)
-        product = scaled.astype(F32) * mixed[p]
+        scaled = (grad_att[p, at, :].astype(F32) * recip[p, at, :]).astype(BF16)
+        product = scaled.astype(F32) * mixed[p, at, :]
         dq = None
         dk = []
         dv = []
@@ -737,115 +735,114 @@
             cut = slice(i * head_width, (i + 1) * head_width)
             delta = jnp.sum(product * head_mask[i], axis=-1, keepdims=True)
             high = delta.astype(BF16).astype(F32)
-            extra = jnp.where(lane == 0, -high, jnp.where(lane == 1, high - delta, 0.0))
+            extra = jnp.where(half_lane == 0, -high, jnp.where(half_lane == 1, high - delta, 0.0))
             grads = scaled * low_mask[i]
             left = jnp.concatenate([grads, extra.astype(BF16)], axis=1)
-            exponent = exps[2 * p + i]
+            exponent = exps[2 * p + i, at, :]
             grad_scores = (exponent.astype(F32) * dot_nt(left, values)).astype(BF16)
             term = dot(grad_scores, keys * low_mask[i])
             dq = term if dq is None else dq + term
             dk.append(dot(turned[cut], grad_scores))
             dv.append(dot(grads.T[cut], exponent))
         dq = (dq * score_scale).astype(BF16)
-        dk = jnp.concatenate(dk, axis=0).astype(BF16).T
-        dv = jnp.concatenate(dv, axis=0).astype(BF16).T
-        for i, block in enumerate((dq, dk, dv)):
-            at = pl.ds(pl.multiple_of(i * side + p * LANES, LANES), LANES)
-            grad_qkv[:, at] = block
-        pool_b[seq, pl.ds(p, 1), :] = jnp.sum(fold_rows(dq.astype(F32)), axis=0, keepdims=True)
-        pool_b[seq, pl.ds(pairs + p, 1), :] = jnp.sum(
-            fold_rows(dv.astype(F32)), axis=0, keepdims=True
-        )
-        return carry
-
-    lax.fori_loop(0, pairs, attend_back, 0, unroll=True)
-    plane_start(pool_b, pb_send, pb_recv)
-
-    plane_wait(pool_a, pa_send, pa_recv)
-    total = pool_a[0]
-    for s in range(1, seq_size):
-        total = total + pool_a[s]
-    z_a[z] = total
-    column_start(z_a, za_send, za_recv)
-
-    def block_at(step):
-        first = step < half_blocks
-        near = jnp.where(first, 1 - z_half, z_half)
-        return near * half_blocks + lax.rem(step, half_blocks)
-
-    def slice_of(block):
-        start = (block - block // half_blocks * half_blocks) * span
-        return pl.ds(pl.multiple_of(start, span), span)
-
-    def part_copy(block):
-        j = block - block // half_blocks * half_blocks
-        at = slice_of(block)
-        return remote(
-            part_out.at[at], part_in.at[at], part_send.at[j], part_recv.at[j], partner, z
-        )
+        dk = jnp.concatenate(dk, axis=0)
+        dv = jnp.concatenate(dv, axis=0)
+        grad_qkv[at, p * LANES : (p + 1) * LANES] = dq
+        dq_sum = jnp.sum(fold_rows(dq.astype(F32)), axis=0, keepdims=True)
+        if first:
+            key_part[p] = dk
+            value_part[p] = dv
+            z_b[z, p : p + 1, :] = dq_sum
+        else:
+            dk = (dk + key_part[p]).astype(BF16).T
+            dv = (dv + value_part[p]).astype(BF16).T
+            grad_qkv[:, side + p * LANES : side + (p + 1) * LANES] = dk
+            grad_qkv[:, 2 * side + p * LANES : 2 * side + (p + 1) * LANES] = dv
+            z_b[z, p : p + 1, :] += dq_sum
+            z_b[z, pairs + p : pairs + p + 1, :] = jnp.sum(
+                fold_rows(dv.astype(F32)), axis=0, keepdims=True
+            )
+
+    half_lane = lax.broadcasted_iota(jnp.int32, (half, LANES), 1)
+    for p in range(pairs):
+        attend_back(near_rows, p, True)
+    all_peers(0, seq_size, seq, plane_a, True)
+    z_a[z] = total_of(pool_a, range(seq_size))
+    all_peers(0, group, z, column_a, False)
+    lax.fori_loop(0, pairs, gat_wait, 0)
+    for p in range(pairs):
+        attend_back(far_rows, p, False)
+    all_peers(0, group, z, column_b, False)
+
+    def half_of(step):
+        return 1 - z_half if step < 2 else z_half
+
+    def part_copy(c):
+        return remote(part_out.at[c], part_in.at[c], part_send.at[c], part_recv.at[c], partner, z)
+
+    def grad_block(j, c):
+        return (
+            core * half_blocks + j,
+            grad_out.at[c],
+            grad_home.at[:, c],
+            grad_send.at[c],
+            grad_recv.at[c],
+            in_sem.at[3 + c],
+        )
+
+    def token_grad(step):
+        c = step % 2
+        own = half_of(step)
+        at = pl.ds(pl.multiple_of(own * half, half), half)
+        columns = slice(c * side, (c + 1) * side)
+        term = dot_nt(grad_qkv[at, :], m_qkv[columns, :])
+
+        @pl.when(own == core)
+        def _():
+            part[c] = term
+
+        @pl.when(own != core)
+        def _():
+            part_out[c] = term.astype(BF16)
+            part_copy(c).start()
 
     def finish(step):
-        block = block_at(step)
-
-        @pl.when(block // half_blocks == core)
+        c = step % 2
+        columns = slice(c * side, (c + 1) * side)
+
+        @pl.when(half_of(step) == core)
         def _():
-            at = slice_of(block)
-            part_copy(block).wait_recv()
-            total = grad_h[at, :] + part[lax.rem(step, 2)] + part_in[at, :].astype(F32)
-            grad_out[at, :] = total.astype(BF16)
-            home_block(block, grad_out, grad_home, grad_send, grad_recv, in_sem.at[3])
-
-    def token_grad(step, carry):
-        block = block_at(step)
-        term = dot_nt(grad_qkv[rows_of(block), :], m_qkv[...])
-        mine_now = block // half_blocks == core
-
-        @pl.when(mine_now)
-        def _():
-            part[lax.rem(step, 2)] = term
-
-        @pl.when(jnp.logical_not(mine_now))
-        def _():
-            part_out[slice_of(block), :] = term.astype(BF16)
-            part_copy(block).start()
-
-        @pl.when(step > 0)
-        def _():
-            finish(step - 1)
-
-        return carry
-
-    lax.fori_loop(0, group, token_grad, 0)
-    finish(group - 1)
-
-    def part_wait(j, carry):
-        part_copy(far * half_blocks + j).wait_send()
-        return carry
-
-    lax.fori_loop(0, half_blocks, part_wait, 0)
-
-    plane_wait(pool_b, pb_send, pb_recv)
+            part_copy(c).wait_recv()
+            total = grad_h[:, columns] + part[c] + part_in[c].astype(F32)
+            grad_out[c] = total.astype(BF16)
+            for j in range(half_blocks):
+                home_block(*grad_block(j, c))
+
+    token_grad(0)
+    token_grad(1)
+    finish(0)
+    all_peers(0, group, z, column_a, True)
+    sums_a[own_slice] = total_of(z_a, range(group))
+    all_peers(seq - own_slice, slices, seq, gather_a, False)
+    finish(1)
+    token_grad(2)
+    token_grad(3)
+    finish(2)
+    all_peers(0, group, z, column_b, True)
+    pool_b[seq] = total_of(z_b, range(group))
+    all_peers(0, seq_size, seq, plane_b, False)
+    finish(3)
+
+    for c in range(2):
+        part_copy(c).wait_send()
+    all_peers(seq - own_slice, slices, seq, gather_a, True)
+    all_peers(0, seq_size, seq, plane_b, True)
     for i in range(2):
-        total = pool_b[i]
-        for s in range(2 + i, seq_size, 2):
-            total = total + pool_b[s]
-        z_b[z, i] = total
-    column_start(z_b, zb_send, zb_recv)
-
-    column_wait(z_a, za_send, za_recv)
-    total = z_a[0]
-    for s in range(1, group):
-        total = total + z_a[s]
-    sums_a[...] = total
-
-    column_wait(z_b, zb_send, zb_recv)
-    total = z_b[0]
-    for s in range(1, group):
-        total = total + z_b[s]
-    sums_b[...] = total
-
+        sums_b[i] = total_of(pool_b, range(i, seq_size, 2))
+    spread_done(cotangent, cot, cot_at, cot_send, cot_recv)
     home_done(layer_out, layer_home, lay_send, lay_recv, in_sem.at[2])
-    home_done(grad_out, grad_home, grad_send, grad_recv, in_sem.at[3])
+    for c in range(2):
+        home_done(*grad_block(0, c)[1:])
 
 
 def finish_kernel(
@@ -867,12 +864,13 @@
     inner_line,
     sems,
 ):
-    rows = layer.shape[0]
-    width = layer.shape[2]
+    rows, span, width = layer.shape
+    slices, _, slice_width = sums_a.shape
     copies = [pltpu.make_async_copy(layer, layer_out, sems.at[0])]
     copies[0].start()
     for r in range(rows):
-        wide[r] = grad[r].astype(F32)
+        for c in range(2):
+            wide[r, :, c * width // 2 : (c + 1) * width // 2] = grad[r, c].astype(F32)
         copies.append(pltpu.make_async_copy(wide.at[r], input_grad.at[r], sems.at[1 + r]))
         copies[-1].start()
     pairs = sums_b.shape[1] // 2
@@ -881,9 +879,13 @@
             column = (i * pairs + p) * LANES
             lines[0, :, column : column + LANES] = sums_b[i, p : p + 1, :]
             lines[1, :, column : column + LANES] = sums_b[i, pairs + p : pairs + p + 1, :]
-    for i in range(4):
-        lines[2 + i] = sums_a[i : i + 1, :]
-        inner_line[:, i * width : (i + 1) * width] = sums_a[4 + i : 5 + i, :]
+    for j in range(slices):
+        column = j * slice_width
+        for i in range(4):
+            lines[2 + i, :, column : column + slice_width] = sums_a[j, i : i + 1, :]
+            inner_line[:, i * width + column : i * width + column + slice_width] = sums_a[
+                j, 4 + i : 5 + i, :
+            ]
     targets = (
         grad_bias_query,
         grad_bias_value,
@@ -932,6 +934,8 @@
     side = width // 2
     pairs = side // LANES
     chunks = hidden // FF_CHUNK
+    slices = min(8, seq_size)
+    slice_width = width // slices
     if rows * 2 != group or pairs != 4 or hidden != 4 * width or slots != FF_CHUNK:
         raise ValueError("unsupported sizes")
 
@@ -978,18 +982,22 @@
         pltpu.VMEM((pairs, slots, LANES), BF16),
         pltpu.VMEM((pairs, half, LANES), BF16),
         pltpu.VMEM((slots, 3 * side), BF16),
-        pltpu.VMEM((2, span, width), F32),
+        pltpu.VMEM((pairs, LANES, slots), F32),
+        pltpu.VMEM((pairs, LANES, slots), F32),
+        pltpu.VMEM((slots, LANES), BF16),
+        pltpu.VMEM((2, half, side), F32),
+        pltpu.VMEM((2, half, side), BF16),
+        pltpu.VMEM((2, half, side), BF16),
+        pltpu.VMEM((2, half, side), BF16),
         pltpu.VMEM((half, width), BF16),
-        pltpu.VMEM((half, width), BF16),
-        pltpu.VMEM((half, width), BF16),
-        pltpu.VMEM((half, width), BF16),
-        pltpu.VMEM((seq_size, 8, width), F32),
-        pltpu.VMEM((group, 8, width), F32),
+        pltpu.VMEM((8, width), F32),
+        pltpu.VMEM((seq_size, 8, slice_width), F32),
+        pltpu.VMEM((group, 8, slice_width), F32),
         pltpu.VMEM((seq_size, 8, LANES), F32),
-        pltpu.VMEM((group, 2, 8, LANES), F32),
+        pltpu.VMEM((group, 8, LANES), F32),
         dma((5 + 2 * chunks,)),
         dma((9,)),
-        dma((4,)),
+        dma((5,)),
         dma((rows,)),
         dma((half_blocks,)),
         dma((half_blocks,)),
@@ -1003,14 +1011,16 @@
         dma((pairs,)),
         dma((half_blocks,)),
         dma((rows,)),
-        dma((half_blocks,)),
-        dma((half_blocks,)),
-        dma((half_blocks,)),
-        dma((rows,)),
+        dma((2,)),
+        dma((2,)),
+        dma((2, half_blocks)),
+        dma((2, rows)),
         dma((seq_size,)),
         dma((seq_size,)),
         dma((group,)),
         dma((group,)),
+        dma((slices,)),
+        dma((slices,)),
         dma((seq_size,)),
         dma((seq_size,)),
         dma((group,)),
@@ -1031,8 +1041,8 @@
         functools.partial(kernel, seq_size, group),
         out_shape=(
             pltpu.VMEM(tokens.shape, BF16),
-            pltpu.VMEM(tokens.shape, BF16),
-            pltpu.VMEM((8, width), F32),
+            pltpu.VMEM((rows, 2, span, side), BF16),
+            pltpu.VMEM((slices, 8, slice_width), F32),
             pltpu.VMEM((2, 8, LANES), F32),
         ),
         in_specs=[any_space] * 2 + [smem] * 2 + [any_space] * (6 + len(vectors)),

time: 66.3 us -> 62.3 us (0.940)
  the two profiles are of different devices: /device:TPU:0 before, /device:TPU:9 now
where the time goes in v2:
time: 62.3 us; the launch traced here: 62.2 us
  Pallas kernels  61.3 us (98%)
  between operations  0.82 us (1%)
    pallas_call x1, Pallas kernels, per_device(): pl.pallas_call(functools.partial(kernel, seq_size, group), out_shape=(plt...  60.1 us

profile of v2, /device:TPU:9, one launch (start us, length us, event | category | flops | bytes accessed | tf_op | source)
XLA Modules:
  0.0 62.2 jit_solution(17398696729199926806)
XLA Ops:
  0.7 60.1 %shard_map.250 = (bf16[2,128,1024]{2,1,0:T(8,128)(2,1)S(1)}, bf16[2,2,128,512]{3,2,1,0:T(8,128)(2,1)S(1)}, f32[8,8,128]{2,1,0:T(8,128)S(1)}, f32[2,8,128]{2,1,0:T(8,128)S(1)}) custom-call(bf16[2,128,1024]{2,1,0:T(8,128)(2,1)} %tokens.1, bf16[2,128,1024]{2,1,0:T(8,128)(2,1)} %cotangent.1, s32[2,3]{1,0:T(2,128)} %doc_lengths.1, s32[2]{0:T(128)} %pad_counts.1, ...), custom_call_target="tpu_custom_call" | custom-call | tf_op jit(solution)/shard_map/pallas_call | solution.py:1040
  60.8 1.2 %shard_map.251 = (bf16[2,128,1024]{2,1,0:T(8,128)(2,1)}, f32[2,128,1024]{2,1,0:T(8,128)}, f32[1,1024]{1,0:T(1,128)}, f32[1,1024]{1,0:T(1,128)}, f32[1,1024]{1,0:...) custom-call(bf16[2,128,1024]{2,1,0:T(8,128)(2,1)S(1)} %get-tuple-element.22.layer, ...), custom_call_target="tpu_custom_call" | custom-call | tf_op jit(solution)/shard_map/pallas_call | solution.py:1068

commit v3 on v2

v3 whole, which is shorter than its diff:
```python
import functools

import jax
import jax.numpy as jnp
from jax import lax
from jax.experimental import pallas as pl
from jax.experimental.pallas import tpu as pltpu
from jax.sharding import PartitionSpec as P

HEADS = 16
LANES = 128
EPS = 1e-06
BIG = 2.0**30
FF_CHUNK = 512
FEATURE_CHUNK = 256
NORM_ROWS = 32
GRAD_COLUMNS = 512
GRAD_LAG = 1
MESH = pl.DeviceIdType.MESH
F32 = jnp.float32
BF16 = jnp.bfloat16


def dot(left, right):
    return lax.dot_general(left, right, (((1,), (0,)), ((), ())), preferred_element_type=F32)


def dot_nt(left, right):
    return lax.dot_general(left, right, (((1,), (1,)), ((), ())), preferred_element_type=F32)


def dot_tn(left, right):
    return lax.dot_general(left, right, (((0,), (0,)), ((), ())), preferred_element_type=F32)


def normed(hidden):
    row_mean = jnp.mean(hidden, axis=-1, keepdims=True)
    centred = hidden - row_mean
    inv_std = lax.rsqrt(jnp.mean(centred * centred, axis=-1, keepdims=True) + EPS)
    return centred * inv_std, inv_std


def norm_back(gradient, norm, inv_std):
    return inv_std * (
        gradient
        - jnp.mean(gradient, axis=-1, keepdims=True)
        - norm * jnp.mean(gradient * norm, axis=-1, keepdims=True)
    )


def fold_rows(block):
    total = block[0:8]
    for start in range(8, block.shape[0], 8):
        total = total + block[start : start + 8]
    return total


def kernel(
    seq_size,
    group,
    tokens,
    cotangent,
    doc_lengths,
    pad_counts,
    w_query,
    w_key,
    w_value,
    w_out,
    w_inner,
    w_outer,
    in_bias_query,
    in_bias_value,
    in_bias_out,
    in_bias_inner,
    in_bias_outer,
    in_gain_attn,
    in_beta_attn,
    in_gain_final,
    in_beta_final,
    layer_home,
    grad_home,
    sums_a,
    sums_b,
    m_qkv,
    m_out,
    m_inner,
    m_outer,
    vectors,
    bias_inner,
    row,
    cot,
    info,
    qs,
    ks,
    vs,
    exps,
    recip,
    mixed,
    att,
    att_far,
    norm_a,
    inv_a,
    mid,
    mid_low,
    acc,
    slope,
    raw,
    active,
    inner_sum,
    grad_h,
    grad_low,
    grad_att,
    grad_far,
    grad_qkv,
    turned,
    lefts,
    grads_turned,
    grad_scores,
    part,
    part_out,
    part_in,
    grad_out,
    layer_out,
    vec_a,
    pool_a,
    z_a,
    pool_b,
    z_b,
    w_sem,
    in_sem,
    tok_send,
    tok_recv,
    pass_send,
    pass_recv,
    info_sem,
    cot_send,
    cot_recv,
    att_send,
    att_recv,
    gat_send,
    gat_recv,
    lay_send,
    lay_recv,
    part_send,
    part_recv,
    grad_send,
    grad_recv,
    bias_send,
    bias_recv,
):
    rows, span, width = tokens.shape
    half_blocks = group // 2
    slots = span * group
    half = slots // 2
    head_width = width // HEADS
    side = width // 2
    pairs = side // LANES
    chunks = m_inner.shape[0]
    norm_steps = half // NORM_ROWS
    score_scale = head_width**-0.5
    slices = sums_a.shape[0]
    slice_width = width // slices

    seq = lax.axis_index("seq")
    z = lax.axis_index("head")
    core = lax.rem(seq, 2)
    base = seq - core
    partner = base + 1 - core
    z_half = z // half_blocks
    far = 1 - core

    def near_at(j):
        return pl.ds(pl.multiple_of(half + j * span, span), span)

    def far_at(j):
        return pl.ds(pl.multiple_of(j * span, span), span)

    def remote(src, dst, send_sem, recv_sem, at_seq, at_head):
        return pltpu.make_async_remote_copy(
            src_ref=src,
            dst_ref=dst,
            send_sem=send_sem,
            recv_sem=recv_sem,
            device_id=(at_seq, at_head),
            device_id_type=MESH,
        )

    barrier = pltpu.get_barrier_semaphore()

    def greet_z(step, carry):
        pl.semaphore_signal(
            barrier, inc=1, device_id=(seq, lax.rem(z + step, group)), device_id_type=MESH
        )
        return carry

    def greet_seq(step, carry):
        pl.semaphore_signal(
            barrier, inc=1, device_id=(lax.rem(seq + step, seq_size), z), device_id_type=MESH
        )
        return carry

    for r in range(rows):
        target = core * rows + r

        @pl.when(target != z)
        def _():
            pl.semaphore_signal(
                barrier, inc=1, device_id=(base + z_half, target), device_id_type=MESH
            )

    lax.fori_loop(1, seq_size, greet_seq, 0)
    lax.fori_loop(1, group, greet_z, 0)

    mine = pl.ds(pl.multiple_of(core * side, side), side)
    theirs = pl.ds(pl.multiple_of(far * side, side), side)
    for i, weight in enumerate((w_query, w_key, w_value)):
        pltpu.make_async_copy(
            weight.at[:, mine], m_qkv.at[:, i * side : (i + 1) * side], w_sem.at[0]
        ).start()
    for i, vector in enumerate(
        (
            in_bias_query,
            in_bias_value,
            in_bias_out,
            in_bias_outer,
            in_gain_attn,
            in_beta_attn,
            in_gain_final,
            in_beta_final,
        )
    ):
        pltpu.make_async_copy(vector, vectors.at[i], w_sem.at[4]).start()
    pltpu.make_async_copy(in_bias_inner, bias_inner, w_sem.at[5]).start()

    def loaded(target, i):
        pltpu.make_async_copy(target, target, w_sem.at[i]).wait()

    line = lax.broadcasted_iota(jnp.int32, (8, LANES), 0)
    for r in range(rows):
        first = doc_lengths[r, 0]
        second = first + doc_lengths[r, 1]
        third = second + doc_lengths[r, 2]
        ends = jnp.where(line == 0, first, jnp.where(line == 1, second, third))
        info[core, r] = jnp.where(line == 3, slots - pad_counts[r], ends)

    peers = jnp.where(z_half == core, rows - 1, rows)
    pl.semaphore_wait(barrier, peers + seq_size - 1 + group - 1)

    early = (z >= half_blocks // 2) & (z < group - half_blocks // 2)

    def spread(index, source, target_ref, at, send_sem, recv_sem):
        r = jnp.where(core == 0, rows - 1 - index, index)
        target = core * rows + r

        @pl.when(target != z)
        def _():
            remote(
                source.at[r],
                target_ref.at[at],
                send_sem.at[r],
                recv_sem.at[z - z_half * half_blocks],
                base + z_half,
                target,
            ).start()

    def keep(source, target_ref, at, local_sem):
        @pl.when(core == z_half)
        def _():
            pltpu.make_async_copy(
                source.at[z - z_half * rows], target_ref.at[at], local_sem
            ).start()

    def spread_done(index, source, target_ref, at, send_sem, recv_sem):
        r = jnp.where(core == 0, rows - 1 - index, index)
        target = core * rows + r

        @pl.when(target != z)
        def _():
            remote(
                source.at[r],
                target_ref.at[at],
                send_sem.at[r],
                recv_sem.at[z - z_half * half_blocks],
                base + z_half,
                target,
            ).wait_send()

    def arrived(source, target_ref, at, block, send_sem, recv_sem, local_sem):
        j = block - core * half_blocks

        @pl.when(block != z)
        def _():
            remote(
                source.at[0],
                target_ref.at[at],
                send_sem.at[0],
                recv_sem.at[j],
                base + z_half,
                block,
            ).wait_recv()

        @pl.when(block == z)
        def _():
            pltpu.make_async_copy(source.at[0], target_ref.at[at], local_sem).wait()

    info_copy = remote(info.at[core], info.at[core], info_sem.at[0], info_sem.at[1], partner, z)
    info_copy.start()
    tok_at = near_at(z - z_half * half_blocks)
    cot_at = pl.ds(pl.multiple_of((z - z_half * half_blocks) * span, span), span)

    def send_tokens():
        for index in range(rows):
            spread(index, tokens, row, tok_at, tok_send, tok_recv)

    def tokens_sent():
        for index in range(rows):
            spread_done(index, tokens, row, tok_at, tok_send, tok_recv)

    def send_cotangents():
        for index in range(rows):
            spread(index, cotangent, cot, cot_at, cot_send, cot_recv)

    def cotangents_sent():
        for index in range(rows):
            spread_done(index, cotangent, cot, cot_at, cot_send, cot_recv)

    send_tokens()
    keep(tokens, row, tok_at, in_sem.at[0])
    keep(cotangent, cot, cot_at, in_sem.at[1])
    pltpu.make_async_copy(w_out.at[mine], m_out.at[0:side], w_sem.at[1]).start()
    pltpu.make_async_copy(w_out.at[theirs], m_out.at[side:width], w_sem.at[1]).start()
    for f in range(chunks):
        columns = slice(f * FF_CHUNK, (f + 1) * FF_CHUNK)
        pltpu.make_async_copy(w_inner.at[:, columns], m_inner.at[f], w_sem.at[2]).start()
    pltpu.make_async_copy(w_outer, m_outer, w_sem.at[3]).start()

    info_copy.wait_send()
    remote(info.at[far], info.at[far], info_sem.at[0], info_sem.at[1], partner, z).wait_recv()
    loaded(m_qkv, 0)
    loaded(vectors, 4)
    loaded(bias_inner, 5)
    bias_query = vectors[0, :, mine]
    bias_value = vectors[1, :, mine]

    lane = lax.broadcasted_iota(jnp.int32, (slots, LANES), 1)
    place = lax.broadcasted_iota(jnp.int32, (slots, LANES), 0)
    slot = jnp.where(place < half, far * half + place, core * half + place - half)
    ends = info[z_half, z - z_half * rows]
    doc = (slot >= ends[0:1]).astype(jnp.int32)
    for i in range(1, 4):
        doc = doc + (slot >= ends[i : i + 1]).astype(jnp.int32)
    doc_query = jnp.where(doc == lane, BIG, 0.0).astype(BF16)
    doc_key = jnp.where((doc != lane) & (lane < 5), -1.0, 0.0).astype(BF16)
    ones = jnp.ones((slots, LANES), BF16)

    def pass_on(j):
        return remote(
            row.at[near_at(j)], row.at[far_at(j)], pass_send.at[j], pass_recv.at[j], partner, z
        )

    def taken(which, step):
        local = lax.rem(z - z_half * half_blocks + step, half_blocks)
        beyond = jnp.where(z_half == 0, half_blocks - 1 - step, step)
        return jnp.where(which == z_half, local, beyond)

    def project(at):
        x = row[at, :]
        q = (dot(x, m_qkv[:, 0:side]) + bias_query) * score_scale
        k = dot(x, m_qkv[:, side : 2 * side])
        v = dot(x, m_qkv[:, 2 * side : 3 * side]) + bias_value
        for p in range(pairs):
            cut = slice(p * LANES, (p + 1) * LANES)
            qs[p, at, :] = q[:, cut].astype(BF16)
            ks[p, at, :] = k[:, cut].astype(BF16)
            vs[p, at, :] = v[:, cut].astype(BF16)


    def project_step(i, carry):
        in_turn = core == z_half
        own = jnp.where(in_turn, i < half_blocks, lax.rem(i, 2) == 1)
        step = jnp.where(in_turn, lax.rem(i, half_blocks), i // 2)
        j = taken(jnp.where(own, core, far), step)

        @pl.when(own)
        def _():
            block = core * half_blocks + j
            arrived(tokens, row, near_at(j), block, tok_send, tok_recv, in_sem.at[0])
            pass_on(j).start()

            @pl.when((i == group - 1) & jnp.logical_not(early))
            def _():
                send_cotangents()

        @pl.when(jnp.logical_not(own))
        def _():
            pass_on(j).wait_recv()

        project(pl.ds(pl.multiple_of(jnp.where(own, half, 0) + j * span, span), span))
        return carry

    lax.fori_loop(0, group, project_step, 0)

    @pl.when((core == z_half) & jnp.logical_not(early))
    def _():
        send_cotangents()

    for i, target in enumerate((m_out, m_inner, m_outer)):
        loaded(target, 1 + i)

    lane_row = lax.broadcasted_iota(jnp.int32, (1, LANES), 1)
    head_mask = [
        (lane_row < head_width).astype(F32),
        (lane_row >= head_width).astype(F32),
    ]
    low_mask = [mask.astype(BF16) for mask in head_mask]
    near_rows = slice(half, slots)
    far_rows = slice(0, half)

    def score(unit, spot):
        head, at = unit
        p = head // 2
        left = jnp.concatenate([qs[p, at, :] * low_mask[head % 2], doc_query[at, :]], axis=1)
        keys = jnp.concatenate([ks[p], doc_key], axis=1)
        slope[spot, 0:half, :] = dot_nt(left, keys)

    def soften(unit, spot):
        head, at = unit
        scores = slope[spot, 0:half, :]
        exponent = jnp.exp(scores - jnp.max(scores, axis=-1, keepdims=True))
        exps[head, at, :] = exponent.astype(BF16)

    def mix(unit):
        head, at = unit
        both = dot(exps[head, at, :], jnp.concatenate([vs[head // 2], ones], axis=1))
        share = 1.0 / both[:, LANES:]
        return both[:, :LANES] * share * head_mask[head % 2], share * head_mask[head % 2]

    units = [(head, at) for at in (far_rows, near_rows) for head in range(2 * pairs)]
    spots = slope.shape[0]
    score(units[0], 0)
    for i in range(len(units) + 1):
        if i + 1 < len(units):
            score(units[i + 1], (i + 1) % spots)
        if i > 0:
            head, at = units[i - 1]
            if head % 2 == 0:
                held = mix(units[i - 1])
            else:
                total, shares = (a + b for a, b in zip(held, mix(units[i - 1])))
                p = head // 2
                mixed[p, at, :] = total
                recip[p, at, :] = shares
                att[p, at, :] = total.astype(BF16)
        if i < len(units):
            soften(units[i], i % spots)
        if i == 2 * pairs:
            att_copy = remote(
                att.at[:, far_rows], att_far, att_send.at[0], att_recv.at[0], partner, z
            )
            att_copy.start()

            @pl.when(early)
            def _():
                tokens_sent()
                send_cotangents()


    left = jnp.concatenate([att[p, near_rows, :] for p in range(pairs)], axis=1)
    acc[...] = dot(left, m_out[0:side, :])

    def whole(source, target, send_sem, recv_sem):
        return remote(source, target, send_sem, recv_sem, partner, z)

    att_copy.wait()
    left = jnp.concatenate([att_far[p] for p in range(pairs)], axis=1)
    acc[...] += dot(left, m_out[side:width, :])

    def lines_of(step):
        return pl.ds(pl.multiple_of(step * NORM_ROWS, NORM_ROWS), NORM_ROWS)

    def norm_first(step, carry):
        at = lines_of(step)
        near = pl.ds(pl.multiple_of(half + step * NORM_ROWS, NORM_ROWS), NORM_ROWS)
        hidden = row[near, :].astype(F32) + acc[at, :] + vectors[2]
        norm, inv_std = normed(hidden)
        norm_a[at, :] = norm
        inv_a[at, :] = jnp.broadcast_to(inv_std, (NORM_ROWS, LANES))
        middle = norm * vectors[4] + vectors[5]
        mid[at, :] = middle
        mid_low[at, :] = middle.astype(BF16)
        return carry

    lax.fori_loop(0, norm_steps, norm_first, 0, unroll=True)

    def slope_at(f):
        return f // 2, slice(f % 2 * half, (f % 2 + 1) * half)

    def activate(f):
        columns = slice(f * FF_CHUNK, (f + 1) * FF_CHUNK)
        inner = raw[f % 2] + bias_inner[:, columns]
        cdf = 0.5 * (1.0 + lax.erf(inner * 0.7071067811865476))
        which, lines = slope_at(f)
        slope[which, lines, :] = cdf + inner * jnp.exp(-0.5 * inner * inner) * 0.3989422804014327
        active[:, columns] = (inner * cdf).astype(BF16)

    raw[0] = dot(mid_low[...], m_inner[0])
    for f in range(chunks):
        if f + 1 < chunks:
            raw[(f + 1) % 2] = dot(mid_low[...], m_inner[f + 1])
        activate(f)
    for n in range(0, width, FEATURE_CHUNK):
        acc[:, n : n + FEATURE_CHUNK] = dot(active[...], m_outer[:, n : n + FEATURE_CHUNK])

    def cot_wait(j, carry):
        at = pl.ds(pl.multiple_of(j * span, span), span)
        arrived(cotangent, cot, at, core * half_blocks + j, cot_send, cot_recv, in_sem.at[1])
        return carry

    lax.fori_loop(0, half_blocks, cot_wait, 0)

    live_end = ends[3:4, 0:1]
    zero_sum = jnp.zeros((8, width), F32)

    def norm_last(step, carry):
        beta_sum, outer_sum = carry
        at = lines_of(step)
        hidden = mid[at, :] + acc[at, :] + vectors[3]
        norm, inv_std = normed(hidden)
        place = lax.broadcasted_iota(jnp.int32, (NORM_ROWS, 1), 0) + core * half + step * NORM_ROWS
        live = (place < live_end).astype(F32)
        layer_out[at, :] = (live * (norm * vectors[6] + vectors[7])).astype(BF16)
        grad_final = live * cot[at, :].astype(F32)
        grad_hidden = norm_back(grad_final * vectors[6], norm, inv_std)
        grad_h[at, :] = grad_hidden
        grad_low[at, :] = grad_hidden.astype(BF16)
        return beta_sum + fold_rows(grad_final), outer_sum + fold_rows(grad_hidden)

    def home_block(block, source, target_ref, send_sem, recv_sem, local_sem):
        j = block - core * half_blocks
        src = source.at[pl.ds(pl.multiple_of(j * span, span), span)]
        line_at = z - z_half * rows

        @pl.when(block != z)
        def _():
            remote(
                src,
                target_ref.at[line_at],
                send_sem.at[j],
                recv_sem.at[line_at],
                base + z_half,
                block,
            ).start()

        @pl.when(block == z)
        def _():
            pltpu.make_async_copy(src, target_ref.at[line_at], local_sem).start()

    def home_done(source, target_ref, send_sem, recv_sem, local_sem):
        for j in range(half_blocks):
            block = core * half_blocks + j
            src = source.at[j * span : (j + 1) * span]
            line_at = z - z_half * rows

            @pl.when(block != z)
            def _():
                remote(
                    src,
                    target_ref.at[line_at],
                    send_sem.at[j],
                    recv_sem.at[line_at],
                    base + z_half,
                    block,
                ).wait_send()

            @pl.when(block == z)
            def _():
                pltpu.make_async_copy(src, target_ref.at[line_at], local_sem).wait()

        for r in range(rows):
            target = core * rows + r

            @pl.when(target != z)
            def _():
                remote(
                    source.at[0:span],
                    target_ref.at[r],
                    send_sem.at[0],
                    recv_sem.at[r],
                    base + z_half,
                    target,
                ).wait_recv()

    sums = lax.fori_loop(0, norm_steps, norm_last, (zero_sum, zero_sum), unroll=True)
    for j in range(half_blocks):
        home_block(
            core * half_blocks + j, layer_out, layer_home, lay_send, lay_recv, in_sem.at[2]
        )
    beta_final_sum, outer_sum = sums

    for f in range(chunks):
        which, lines = slope_at(f)
        columns = slice(f * FF_CHUNK, (f + 1) * FF_CHUNK)
        grad_active = dot_nt(grad_low[...], m_outer[columns, :])
        grad_inner = (grad_active * slope[which, lines, :]).astype(BF16)
        active[:, columns] = grad_inner
        inner_sum[f] = fold_rows(grad_inner.astype(F32))
    for n in range(0, width, FEATURE_CHUNK):
        total = None
        for f in range(chunks):
            term = dot_nt(
                active[:, f * FF_CHUNK : (f + 1) * FF_CHUNK], m_inner[f, n : n + FEATURE_CHUNK, :]
            )
            total = term if total is None else total + term
        acc[:, n : n + FEATURE_CHUNK] = total
    def norm_first_back(step, carry):
        beta_sum, out_sum = carry
        at = lines_of(step)
        grad_middle = grad_h[at, :] + acc[at, :]
        grad_hidden = norm_back(grad_middle * vectors[4], norm_a[at, :], inv_a[at, 0:1])
        grad_h[at, :] = grad_hidden
        grad_low[at, :] = grad_hidden.astype(BF16)
        return beta_sum + fold_rows(grad_middle), out_sum + fold_rows(grad_hidden)

    beta_attn_sum, out_sum = lax.fori_loop(
        0, norm_steps, norm_first_back, (zero_sum, zero_sum), unroll=True
    )

    def sum_up():
        per_line = width // FF_CHUNK
        for f in range(chunks):
            line_at = 4 + f // per_line
            column = f % per_line * FF_CHUNK
            vec_a[line_at : line_at + 1, column : column + FF_CHUNK] = jnp.sum(
                inner_sum[f], axis=0, keepdims=True
            )
        for i, lines in enumerate((out_sum, outer_sum, beta_attn_sum, beta_final_sum)):
            vec_a[i : i + 1, :] = jnp.sum(lines, axis=0, keepdims=True)
        pool_a[seq] = vec_a[:, pl.ds(pl.multiple_of(own_slice * slice_width, LANES), slice_width)]

    def send_all(start, size, here, make):
        def go(step, carry):
            make(start + lax.rem(here - start + step, size)).start()
            return carry

        lax.fori_loop(1, size, go, 0)

    def wait_all(pool, size, make):
        everything = pool.at[pl.ds(0, size - 1)]
        copy = make(everything, everything)
        copy.wait()

    def bias_copy(i, peer_seq, peer_z):
        return lambda source, target: remote(
            source, target, bias_send.at[i], bias_recv.at[i], peer_seq, peer_z
        )

    def plane_a(peer):
        piece = pl.ds(pl.multiple_of(lax.rem(peer, slices) * slice_width, LANES), slice_width)
        return bias_copy(0, peer, z)(vec_a.at[:, piece], pool_a.at[seq])

    def column_a(peer):
        return bias_copy(1, seq, peer)(z_a.at[z], z_a.at[z])

    own_slice = lax.rem(seq, slices)

    def gather_a(peer):
        return bias_copy(2, peer, z)(sums_a.at[own_slice], sums_a.at[own_slice])

    def column_b(peer):
        return bias_copy(3, seq, peer)(z_b.at[z], z_b.at[z])

    def plane_b(peer):
        return bias_copy(4, peer, z)(pool_b.at[seq], pool_b.at[seq])

    def total_of(pool, places):
        total = pool[places[0]]
        for place in places[1:]:
            total = total + pool[place]
        return total

    def gat_copy(p):
        return remote(
            grad_far.at[p], grad_att.at[p, far_rows], gat_send.at[0], gat_recv.at[0], partner, z
        )

    lines = dot_nt(grad_low[...], m_out[side:width, :])
    for p in range(pairs):
        grad_far[p] = lines[:, p * LANES : (p + 1) * LANES].astype(BF16)
        gat_copy(p).start()
    lines = dot_nt(grad_low[...], m_out[0:side, :])
    for p in range(pairs):
        grad_att[p, near_rows, :] = lines[:, p * LANES : (p + 1) * LANES].astype(BF16)
        turned[p] = qs[p].T

    def prepare(p, at):
        scaled = (grad_att[p, at, :].astype(F32) * recip[p, at, :]).astype(BF16)
        product = scaled.astype(F32) * mixed[p, at, :]
        half_lane = lane[at, :]
        for i in range(2):
            delta = jnp.sum(product * head_mask[i], axis=-1, keepdims=True)
            high = delta.astype(BF16).astype(F32)
            extra = jnp.where(half_lane == 0, -high, jnp.where(half_lane == 1, high - delta, 0.0))
            grads = scaled * low_mask[i]
            lefts[2 * p + i, at, :] = jnp.concatenate([grads, extra.astype(BF16)], axis=1)
            cut = slice(i * head_width, (i + 1) * head_width)
            grads_turned[p, cut, at] = grads.T[cut]

    def score_grads(p):
        values = jnp.concatenate([vs[p], ones], axis=1)
        for i in range(2):
            head = 2 * p + i
            grad_probs = dot_nt(lefts[head], values)
            grad_scores[head % 4] = (exps[head].astype(F32) * grad_probs).astype(BF16)

    def attend_back(p):
        dq = None
        dk = []
        dv = []
        for i in range(2):
            cut = slice(i * head_width, (i + 1) * head_width)
            head = 2 * p + i
            term = dot(grad_scores[head % 4], ks[p] * low_mask[i])
            dq = term if dq is None else dq + term
            dk.append(dot(turned[p, cut, :], grad_scores[head % 4]))
            dv.append(dot(grads_turned[p, cut, :], exps[head]))
        dq = (dq * score_scale).astype(BF16)
        dk = jnp.concatenate(dk, axis=0).astype(BF16).T
        dv = jnp.concatenate(dv, axis=0).astype(BF16).T
        for i, block in enumerate((dq, dk, dv)):
            grad_qkv[:, i * side + p * LANES : i * side + (p + 1) * LANES] = block
        z_b[z, p : p + 1, :] = jnp.sum(fold_rows(dq.astype(F32)), axis=0, keepdims=True)
        z_b[z, pairs + p : pairs + p + 1, :] = jnp.sum(
            fold_rows(dv.astype(F32)), axis=0, keepdims=True
        )

    sum_up()
    send_all(0, seq_size, seq, plane_a)
    for p in range(pairs):
        prepare(p, near_rows)
    whole(grad_far, grad_far, gat_send.at[0], gat_recv.at[0]).wait()
    for p in range(pairs):
        prepare(p, far_rows)
    score_grads(0)
    for p in range(pairs):
        if p + 1 < pairs:
            score_grads(p + 1)
        attend_back(p)
    send_all(0, group, z, column_b)
    wait_all(pool_a, seq_size, bias_copy(0, partner, z))
    z_a[z] = total_of(pool_a, range(seq_size))
    send_all(0, group, z, column_a)

    def part_copy(c, j):
        at = far_at(j)
        return remote(
            part_out.at[c, at], part_in.at[c, at], part_send.at[c, j], part_recv.at[c, j], partner, z
        )

    def token_grad(first, c):
        mine_now = core == (1 - z_half if first else z_half)
        at = pl.ds(pl.multiple_of(jnp.where(mine_now, half, 0), half), half)
        columns = slice(c * GRAD_COLUMNS, (c + 1) * GRAD_COLUMNS)
        term = dot_nt(grad_qkv[at, :], m_qkv[columns, :])

        @pl.when(mine_now)
        def _():
            part[c] = term

        @pl.when(jnp.logical_not(mine_now))
        def _():
            for j in range(half_blocks):
                at = slice(j * span, (j + 1) * span)
                part_out[c, at, :] = term[at].astype(BF16)
                part_copy(c, j).start()

    home_line = z - z_half * rows

    def finish(first, c):
        columns = slice(c * GRAD_COLUMNS, (c + 1) * GRAD_COLUMNS)

        @pl.when(core == (1 - z_half if first else z_half))
        def _():
            for j in range(half_blocks):
                block = core * half_blocks + j
                at = slice(j * span, (j + 1) * span)
                part_copy(c, j).wait_recv()
                total = grad_h[at, columns] + part[c, at, :] + part_in[c, at, :].astype(F32)
                grad_out[c, at, :] = total.astype(BF16)
                source = grad_out.at[c, at]

                @pl.when(block != z)
                def _():
                    remote(
                        source,
                        grad_home.at[home_line, c],
                        grad_send.at[j],
                        grad_recv.at[home_line],
                        base + z_half,
                        block,
                    ).start()

                @pl.when(block == z)
                def _():
                    pltpu.make_async_copy(source, grad_home.at[home_line, c], in_sem.at[3]).start()

    def grads_done():
        for j in range(half_blocks):
            block = core * half_blocks + j
            everything = grad_home.at[home_line]

            @pl.when(block != z)
            def _():
                whole(everything, everything, grad_send.at[j], grad_recv.at[home_line]).wait_send()

            @pl.when(block == z)
            def _():
                pltpu.make_async_copy(everything, everything, in_sem.at[3]).wait()

        for r in range(rows):

            @pl.when(core * rows + r != z)
            def _():
                everything = grad_home.at[r]
                whole(everything, everything, grad_send.at[0], grad_recv.at[r]).wait_recv()

    pieces = part.shape[0]
    for first in (True, False):
        for c in range(pieces):
            token_grad(first, c)
            if c >= GRAD_LAG:
                finish(first, c - GRAD_LAG)
        for c in range(pieces - GRAD_LAG, pieces):
            finish(first, c)
    wait_all(z_a, group, bias_copy(1, partner, z))
    sums_a[own_slice] = total_of(z_a, range(group))
    send_all(seq - own_slice, slices, seq, gather_a)
    wait_all(z_b, group, bias_copy(3, partner, z))
    pool_b[seq] = total_of(z_b, range(group))
    send_all(0, seq_size, seq, plane_b)

    for c in range(pieces):
        for j in range(half_blocks):
            part_copy(c, j).wait_send()
    wait_all(sums_a, slices, bias_copy(2, partner, z))
    wait_all(pool_b, seq_size, bias_copy(4, partner, z))
    for i in range(2):
        sums_b[i] = total_of(pool_b, range(i, seq_size, 2))

    @pl.when(jnp.logical_not(early))
    def _():
        tokens_sent()

    cotangents_sent()

    def pass_wait(j, carry):
        pass_on(j).wait_send()
        return carry

    lax.fori_loop(0, half_blocks, pass_wait, 0)
    home_done(layer_out, layer_home, lay_send, lay_recv, in_sem.at[2])
    grads_done()


def finish_kernel(
    layer,
    grad,
    sums_a,
    sums_b,
    layer_out,
    input_grad,
    grad_bias_query,
    grad_bias_value,
    grad_bias_out,
    grad_bias_inner,
    grad_bias_outer,
    grad_beta_attn,
    grad_beta_final,
    wide,
    lines,
    inner_line,
    sems,
):
    rows, span, width = layer.shape
    slices, _, slice_width = sums_a.shape
    copies = [pltpu.make_async_copy(layer, layer_out, sems.at[0])]
    copies[0].start()
    for r in range(rows):
        for c in range(grad.shape[1]):
            wide[r, :, c * GRAD_COLUMNS : (c + 1) * GRAD_COLUMNS] = grad[r, c].astype(F32)
        copies.append(pltpu.make_async_copy(wide.at[r], input_grad.at[r], sems.at[1 + r]))
        copies[-1].start()
    pairs = sums_b.shape[1] // 2
    for i in range(2):
        for p in range(pairs):
            column = (i * pairs + p) * LANES
            lines[0, :, column : column + LANES] = sums_b[i, p : p + 1, :]
            lines[1, :, column : column + LANES] = sums_b[i, pairs + p : pairs + p + 1, :]
    for j in range(slices):
        column = j * slice_width
        for i in range(4):
            lines[2 + i, :, column : column + slice_width] = sums_a[j, i : i + 1, :]
            inner_line[:, i * width + column : i * width + column + slice_width] = sums_a[
                j, 4 + i : 5 + i, :
            ]
    targets = (
        grad_bias_query,
        grad_bias_value,
        grad_bias_out,
        grad_bias_outer,
        grad_beta_attn,
        grad_beta_final,
    )
    for i, target in enumerate(targets):
        copies.append(pltpu.make_async_copy(lines.at[i], target, sems.at[1 + rows + i]))
        copies[-1].start()
    copies.append(pltpu.make_async_copy(inner_line, grad_bias_inner, sems.at[7 + rows]))
    copies[-1].start()
    for copy in copies:
        copy.wait()


def per_device(
    seq_size,
    group,
    tokens,
    doc_lengths,
    pad_counts,
    w_query,
    w_key,
    w_value,
    w_out,
    w_inner,
    w_outer,
    bias_query,
    bias_value,
    bias_out,
    bias_inner,
    bias_outer,
    gain_attn,
    beta_attn,
    gain_final,
    beta_final,
    cotangent,
):
    rows, span, width = tokens.shape
    hidden = w_inner.shape[1]
    slots = span * group
    half = slots // 2
    half_blocks = group // 2
    side = width // 2
    pairs = side // LANES
    chunks = hidden // FF_CHUNK
    slices = min(8, seq_size)
    pieces = width // GRAD_COLUMNS
    slice_width = width // slices
    if rows * 2 != group or pairs != 4 or hidden != 4 * width or slots != FF_CHUNK:
        raise ValueError("unsupported sizes")

    any_space = pl.BlockSpec(memory_space=pl.ANY)
    vmem = pl.BlockSpec(memory_space=pltpu.VMEM)
    smem = pl.BlockSpec(memory_space=pltpu.SMEM)
    dma = pltpu.SemaphoreType.DMA
    scratch = [
        pltpu.VMEM((width, 3 * side), BF16),
        pltpu.VMEM((width, width), BF16),
        pltpu.VMEM((chunks, width, FF_CHUNK), BF16),
        pltpu.VMEM((hidden, width), BF16),
        pltpu.VMEM((8, 1, width), F32),
        pltpu.VMEM((1, hidden), F32),
        pltpu.VMEM((slots, width), BF16),
        pltpu.VMEM((half, width), BF16),
        pltpu.VMEM((2, rows, 8, LANES), jnp.int32),
        pltpu.VMEM((pairs, slots, LANES), BF16),
        pltpu.VMEM((pairs, slots, LANES), BF16),
        pltpu.VMEM((pairs, slots, LANES), BF16),
        pltpu.VMEM((2 * pairs, slots, slots), BF16),
        pltpu.VMEM((pairs, slots, LANES), F32),
        pltpu.VMEM((pairs, slots, LANES), F32),
        pltpu.VMEM((pairs, slots, LANES), BF16),
        pltpu.VMEM((pairs, half, LANES), BF16),
        pltpu.VMEM((half, width), F32),
        pltpu.VMEM((half, LANES), F32),
        pltpu.VMEM((half, width), F32),
        pltpu.VMEM((half, width), BF16),
        pltpu.VMEM((half, width), F32),
        pltpu.VMEM((chunks // 2, slots, slots), F32),
        pltpu.VMEM((2, half, FF_CHUNK), F32),
        pltpu.VMEM((half, hidden), BF16),
        pltpu.VMEM((chunks, 8, FF_CHUNK), F32),
        pltpu.VMEM((half, width), F32),
        pltpu.VMEM((half, width), BF16),
        pltpu.VMEM((pairs, slots, LANES), BF16),
        pltpu.VMEM((pairs, half, LANES), BF16),
        pltpu.VMEM((slots, 3 * side), BF16),
        pltpu.VMEM((pairs, LANES, slots), BF16),
        pltpu.VMEM((2 * pairs, slots, 2 * LANES), BF16),
        pltpu.VMEM((pairs, LANES, slots), BF16),
        pltpu.VMEM((4, slots, slots), BF16),
        pltpu.VMEM((pieces, half, GRAD_COLUMNS), F32),
        pltpu.VMEM((pieces, half, GRAD_COLUMNS), BF16),
        pltpu.VMEM((pieces, half, GRAD_COLUMNS), BF16),
        pltpu.VMEM((pieces, half, GRAD_COLUMNS), BF16),
        pltpu.VMEM((half, width), BF16),
        pltpu.VMEM((8, width), F32),
        pltpu.VMEM((seq_size, 8, slice_width), F32),
        pltpu.VMEM((group, 8, slice_width), F32),
        pltpu.VMEM((seq_size, 8, LANES), F32),
        pltpu.VMEM((group, 8, LANES), F32),
        dma((6,)),
        dma((4,)),
        dma((rows,)),
        dma((half_blocks,)),
        dma((half_blocks,)),
        dma((half_blocks,)),
        dma((2,)),
        dma((rows,)),
        dma((half_blocks,)),
        dma((1,)),
        dma((1,)),
        dma((1,)),
        dma((1,)),
        dma((half_blocks,)),
        dma((rows,)),
        dma((pieces, half_blocks)),
        dma((pieces, half_blocks)),
        dma((half_blocks,)),
        dma((rows,)),
        dma((5,)),
        dma((5,)),
    ]
    vectors = (
        bias_query,
        bias_value,
        bias_out,
        bias_inner,
        bias_outer,
        gain_attn,
        beta_attn,
        gain_final,
        beta_final,
    )
    layer_home, grad_home, sums_a, sums_b = pl.pallas_call(
        functools.partial(kernel, seq_size, group),
        out_shape=(
            pltpu.VMEM(tokens.shape, BF16),
            pltpu.VMEM((rows, pieces, span, GRAD_COLUMNS), BF16),
            pltpu.VMEM((slices, 8, slice_width), F32),
            pltpu.VMEM((2, 8, LANES), F32),
        ),
        in_specs=[any_space] * 2 + [smem] * 2 + [any_space] * (6 + len(vectors)),
        out_specs=(vmem,) * 4,
        scratch_shapes=scratch,
        compiler_params=pltpu.CompilerParams(
            collective_id=0, has_side_effects=True, vmem_limit_bytes=58 * 2**20
        ),
    )(
        tokens,
        cotangent,
        doc_lengths,
        pad_counts,
        w_query,
        w_key,
        w_value,
        w_out,
        w_inner,
        w_outer,
        *[vector.reshape(1, -1) for vector in vectors],
    )
    line = jax.ShapeDtypeStruct((1, width), F32)
    results = pl.pallas_call(
        finish_kernel,
        out_shape=(
            jax.ShapeDtypeStruct(tokens.shape, BF16),
            jax.ShapeDtypeStruct(tokens.shape, F32),
            line,
            line,
            line,
            jax.ShapeDtypeStruct((1, hidden), F32),
            line,
            line,
            line,
        ),
        in_specs=[vmem] * 4,
        out_specs=(any_space,) * 9,
        scratch_shapes=[
            pltpu.VMEM(tokens.shape, F32),
            pltpu.VMEM((6, 1, width), F32),
            pltpu.VMEM((1, hidden), F32),
            dma((8 + rows,)),
        ],
        compiler_params=pltpu.CompilerParams(vmem_limit_bytes=32 * 2**20),
    )(layer_home, grad_home, sums_a, sums_b)
    return tuple(results[:2]) + tuple(vector.reshape(-1) for vector in results[2:])


def solution(mesh):
    split = P("seq", "head", None)
    placed = (split, P("seq", None), P("seq")) + (P(),) * 15 + (split,)
    return jax.shard_map(
        functools.partial(per_device, mesh.shape["seq"], mesh.shape["head"]),
        mesh=mesh,
        in_specs=placed,
        out_specs=(split, split) + (P(),) * 7,
        check_vma=False,
    )
```

time: 62.3 us -> 58.4 us (0.937)
  the two profiles are of different devices: /device:TPU:9 before, /device:TPU:0 now
where the time goes in v3:
time: 58.4 us; the launch traced here: 57.9 us
  Pallas kernels  57.1 us (98%)
  between operations  0.82 us (1%)
    pallas_call x1, Pallas kernels, per_device(): pl.pallas_call(functools.partial(kernel, seq_size, group), out_shape=(plt...  55.9 us
    pallas_call x1, Pallas kernels, per_device(): pl.pallas_call(finish_kernel, out_shape=(jax.ShapeDtypeStruct(tokens.shap...  1.24 us

profile of v3, /device:TPU:0, one launch (start us, length us, event | category | flops | bytes accessed | tf_op | source)
XLA Modules:
  0.0 57.9 jit_solution(5672715161965021574)
XLA Ops:
  0.7 55.9 %shard_map.250 = (bf16[2,128,1024]{2,1,0:T(8,128)(2,1)S(1)}, bf16[2,2,128,512]{3,2,1,0:T(8,128)(2,1)S(1)}, f32[8,8,128]{2,1,0:T(8,128)S(1)}, f32[2,8,128]{2,1,0:T(8,128)S(1)}) custom-call(bf16[2,128,1024]{2,1,0:T(8,128)(2,1)} %tokens.1, bf16[2,128,1024]{2,1,0:T(8,128)(2,1)} %cotangent.1, s32[2,3]{1,0:T(2,128)} %doc_lengths.1, s32[2]{0:T(128)} %pad_counts.1, ...), custom_call_target="tpu_custom_call" | custom-call | tf_op jit(solution)/shard_map/pallas_call | solution.py:1042
  56.5 1.2 %shard_map.251 = (bf16[2,128,1024]{2,1,0:T(8,128)(2,1)}, f32[2,128,1024]{2,1,0:T(8,128)}, f32[1,1024]{1,0:T(1,128)}, f32[1,1024]{1,0:T(1,128)}, f32[1,1024]{1,0:...) custom-call(bf16[2,128,1024]{2,1,0:T(8,128)(2,1)S(1)} %get-tuple-element.22.layer, ...), custom_call_target="tpu_custom_call" | custom-call | tf_op jit(solution)/shard_map/pallas_call | solution.py:1070

commit v4 on v3

--- a/solution.py
+++ b/solution.py
@@ -12,10 +12,8 @@
 EPS = 1e-06
 BIG = 2.0**30
 FF_CHUNK = 512
-FEATURE_CHUNK = 256
+FEATURE_CHUNK = 512
 NORM_ROWS = 32
-GRAD_COLUMNS = 512
-GRAD_LAG = 1
 MESH = pl.DeviceIdType.MESH
 F32 = jnp.float32
 BF16 = jnp.bfloat16
@@ -100,11 +98,13 @@
     att_far,
     norm_a,
     inv_a,
+    inv_f,
     mid,
     mid_low,
     acc,
     slope,
-    raw,
+    raw_even,
+    raw_odd,
     active,
     inner_sum,
     grad_h,
@@ -199,14 +199,12 @@
         )
         return carry
 
-    for r in range(rows):
-        target = core * rows + r
-
-        @pl.when(target != z)
+    for r in range(half_blocks):
+        other = core * half_blocks + r
+
+        @pl.when(other != z)
         def _():
-            pl.semaphore_signal(
-                barrier, inc=1, device_id=(base + z_half, target), device_id_type=MESH
-            )
+            pl.semaphore_signal(barrier, inc=1, device_id=(partner, other), device_id_type=MESH)
 
     lax.fori_loop(1, seq_size, greet_seq, 0)
     lax.fori_loop(1, group, greet_z, 0)
@@ -243,8 +241,8 @@
         ends = jnp.where(line == 0, first, jnp.where(line == 1, second, third))
         info[core, r] = jnp.where(line == 3, slots - pad_counts[r], ends)
 
-    peers = jnp.where(z_half == core, rows - 1, rows)
-    pl.semaphore_wait(barrier, peers + seq_size - 1 + group - 1)
+    crossed = jnp.where(z_half == core, 0, group - 1)
+    pl.semaphore_wait(barrier, crossed + seq_size - 1 + group - 1)
 
     early = (z >= half_blocks // 2) & (z < group - half_blocks // 2)
 
@@ -395,14 +393,14 @@
         def _():
             pass_on(j).wait_recv()
 
+            @pl.when(in_turn & (i == half_blocks) & jnp.logical_not(early))
+            def _():
+                send_cotangents()
+
         project(pl.ds(pl.multiple_of(jnp.where(own, half, 0) + j * span, span), span))
         return carry
 
     lax.fori_loop(0, group, project_step, 0)
-
-    @pl.when((core == z_half) & jnp.logical_not(early))
-    def _():
-        send_cotangents()
 
     for i, target in enumerate((m_out, m_inner, m_outer)):
         loaded(target, 1 + i)
@@ -465,16 +463,14 @@
                 send_cotangents()
 
 
-    left = jnp.concatenate([att[p, near_rows, :] for p in range(pairs)], axis=1)
-    acc[...] = dot(left, m_out[0:side, :])
-
     def whole(source, target, send_sem, recv_sem):
         return remote(source, target, send_sem, recv_sem, partner, z)
 
     att_copy.wait()
-    left = jnp.concatenate([att_far[p] for p in range(pairs)], axis=1)
-    acc[...] += dot(left, m_out[side:width, :])
-
+    left = jnp.concatenate(
+        [att[p, near_rows, :] for p in range(pairs)] + [att_far[p] for p in range(pairs)], axis=1
+    )
+    acc[...] = dot(left, m_out[...])
     def lines_of(step):
         return pl.ds(pl.multiple_of(step * NORM_ROWS, NORM_ROWS), NORM_ROWS)
 
@@ -497,43 +493,36 @@
 
     def activate(f):
         columns = slice(f * FF_CHUNK, (f + 1) * FF_CHUNK)
-        inner = raw[f % 2] + bias_inner[:, columns]
+        inner = raw[f % 2][...] + bias_inner[:, columns]
         cdf = 0.5 * (1.0 + lax.erf(inner * 0.7071067811865476))
         which, lines = slope_at(f)
         slope[which, lines, :] = cdf + inner * jnp.exp(-0.5 * inner * inner) * 0.3989422804014327
         active[:, columns] = (inner * cdf).astype(BF16)
 
-    raw[0] = dot(mid_low[...], m_inner[0])
+    raw = (raw_even, raw_odd)
+    raw_even[...] = dot(mid_low[...], m_inner[0])
     for f in range(chunks):
         if f + 1 < chunks:
-            raw[(f + 1) % 2] = dot(mid_low[...], m_inner[f + 1])
+            raw[(f + 1) % 2][...] = dot(mid_low[...], m_inner[f + 1])
         activate(f)
     for n in range(0, width, FEATURE_CHUNK):
         acc[:, n : n + FEATURE_CHUNK] = dot(active[...], m_outer[:, n : n + FEATURE_CHUNK])
 
-    def cot_wait(j, carry):
-        at = pl.ds(pl.multiple_of(j * span, span), span)
-        arrived(cotangent, cot, at, core * half_blocks + j, cot_send, cot_recv, in_sem.at[1])
+    live_end = ends[3:4, 0:1]
+
+    def live_at(step):
+        place = lax.broadcasted_iota(jnp.int32, (NORM_ROWS, 1), 0) + core * half + step * NORM_ROWS
+        return (place < live_end).astype(F32)
+
+    def norm_last(step, carry):
+        at = lines_of(step)
+        norm, inv_std = normed(mid[at, :] + acc[at, :] + vectors[3])
+        acc[at, :] = norm
+        inv_f[at, :] = jnp.broadcast_to(inv_std, (NORM_ROWS, LANES))
+        layer_out[at, :] = (live_at(step) * (norm * vectors[6] + vectors[7])).astype(BF16)
         return carry
 
-    lax.fori_loop(0, half_blocks, cot_wait, 0)
-
-    live_end = ends[3:4, 0:1]
-    zero_sum = jnp.zeros((8, width), F32)
-
-    def norm_last(step, carry):
-        beta_sum, outer_sum = carry
-        at = lines_of(step)
-        hidden = mid[at, :] + acc[at, :] + vectors[3]
-        norm, inv_std = normed(hidden)
-        place = lax.broadcasted_iota(jnp.int32, (NORM_ROWS, 1), 0) + core * half + step * NORM_ROWS
-        live = (place < live_end).astype(F32)
-        layer_out[at, :] = (live * (norm * vectors[6] + vectors[7])).astype(BF16)
-        grad_final = live * cot[at, :].astype(F32)
-        grad_hidden = norm_back(grad_final * vectors[6], norm, inv_std)
-        grad_h[at, :] = grad_hidden
-        grad_low[at, :] = grad_hidden.astype(BF16)
-        return beta_sum + fold_rows(grad_final), outer_sum + fold_rows(grad_hidden)
+    lax.fori_loop(0, norm_steps, norm_last, 0, unroll=True)
 
     def home_block(block, source, target_ref, send_sem, recv_sem, local_sem):
         j = block - core * half_blocks
@@ -590,11 +579,32 @@
                     target,
                 ).wait_recv()
 
-    sums = lax.fori_loop(0, norm_steps, norm_last, (zero_sum, zero_sum), unroll=True)
     for j in range(half_blocks):
         home_block(
             core * half_blocks + j, layer_out, layer_home, lay_send, lay_recv, in_sem.at[2]
         )
+    for p in range(pairs):
+        turned[p] = qs[p].T
+
+    def cot_wait(j, carry):
+        at = pl.ds(pl.multiple_of(j * span, span), span)
+        arrived(cotangent, cot, at, core * half_blocks + j, cot_send, cot_recv, in_sem.at[1])
+        return carry
+
+    lax.fori_loop(0, half_blocks, cot_wait, 0)
+
+    zero_sum = jnp.zeros((8, width), F32)
+
+    def norm_last_back(step, carry):
+        beta_sum, outer_sum = carry
+        at = lines_of(step)
+        grad_final = live_at(step) * cot[at, :].astype(F32)
+        grad_hidden = norm_back(grad_final * vectors[6], acc[at, :], inv_f[at, 0:1])
+        grad_h[at, :] = grad_hidden
+        grad_low[at, :] = grad_hidden.astype(BF16)
+        return beta_sum + fold_rows(grad_final), outer_sum + fold_rows(grad_hidden)
+
+    sums = lax.fori_loop(0, norm_steps, norm_last_back, (zero_sum, zero_sum), unroll=True)
     beta_final_sum, outer_sum = sums
 
     for f in range(chunks):
@@ -687,10 +697,11 @@
     for p in range(pairs):
         grad_far[p] = lines[:, p * LANES : (p + 1) * LANES].astype(BF16)
         gat_copy(p).start()
+    sum_up()
+    send_all(0, seq_size, seq, plane_a)
     lines = dot_nt(grad_low[...], m_out[0:side, :])
     for p in range(pairs):
         grad_att[p, near_rows, :] = lines[:, p * LANES : (p + 1) * LANES].astype(BF16)
-        turned[p] = qs[p].T
 
     def prepare(p, at):
         scaled = (grad_att[p, at, :].astype(F32) * recip[p, at, :]).astype(BF16)
@@ -702,135 +713,145 @@
             extra = jnp.where(half_lane == 0, -high, jnp.where(half_lane == 1, high - delta, 0.0))
             grads = scaled * low_mask[i]
             lefts[2 * p + i, at, :] = jnp.concatenate([grads, extra.astype(BF16)], axis=1)
-            cut = slice(i * head_width, (i + 1) * head_width)
-            grads_turned[p, cut, at] = grads.T[cut]
-
-    def score_grads(p):
-        values = jnp.concatenate([vs[p], ones], axis=1)
-        for i in range(2):
-            head = 2 * p + i
-            grad_probs = dot_nt(lefts[head], values)
-            grad_scores[head % 4] = (exps[head].astype(F32) * grad_probs).astype(BF16)
-
-    def attend_back(p):
+        grads_turned[p, :, at] = scaled.T
+
+    def score_grads(head, at):
+        values = jnp.concatenate([vs[head // 2], ones], axis=1)
+        grads = exps[head, at, :].astype(F32) * dot_nt(lefts[head, at, :], values)
+        grad_scores[head, at, :] = grads.astype(BF16)
+        return fold_rows(grads)
+
+    def attend_back(p, turn):
+        start = jnp.where(core == (1 - z_half if turn == 0 else z_half), half, 0)
+        part_of = pl.ds(pl.multiple_of(start, half), half)
         dq = None
         dk = []
         dv = []
         for i in range(2):
             cut = slice(i * head_width, (i + 1) * head_width)
             head = 2 * p + i
-            term = dot(grad_scores[head % 4], ks[p] * low_mask[i])
+            term = dot(grad_scores[head, part_of, :], ks[p] * low_mask[i])
             dq = term if dq is None else dq + term
-            dk.append(dot(turned[p, cut, :], grad_scores[head % 4]))
-            dv.append(dot(grads_turned[p, cut, :], exps[head]))
+            dk.append(dot(turned[p, cut, :], grad_scores[head, :, part_of]))
+            dv.append(dot(grads_turned[p, cut, :], exps[head, :, part_of]))
         dq = (dq * score_scale).astype(BF16)
         dk = jnp.concatenate(dk, axis=0).astype(BF16).T
         dv = jnp.concatenate(dv, axis=0).astype(BF16).T
         for i, block in enumerate((dq, dk, dv)):
-            grad_qkv[:, i * side + p * LANES : i * side + (p + 1) * LANES] = block
-        z_b[z, p : p + 1, :] = jnp.sum(fold_rows(dq.astype(F32)), axis=0, keepdims=True)
+            grad_qkv[turn, :, i * side + p * LANES : i * side + (p + 1) * LANES] = block
+
+    def score_grads_of(at):
+        sums = []
+        prepare(0, at)
+        for p in range(pairs):
+            if p + 1 < pairs:
+                prepare(p + 1, at)
+            sums += [score_grads(2 * p, at), score_grads(2 * p + 1, at)]
+        return sums
+
+    near_sums = score_grads_of(near_rows)
+    whole(grad_far, grad_far, gat_send.at[0], gat_recv.at[0]).wait()
+    far_sums = score_grads_of(far_rows)
+    for p in range(pairs):
+        rows_of_pair = []
+        for head in (2 * p, 2 * p + 1):
+            sums = near_sums[head] + far_sums[head]
+            high = sums.astype(BF16)
+            rows_of_pair += [high, (sums - high.astype(F32)).astype(BF16)]
+        query_sum = dot(jnp.concatenate(rows_of_pair, axis=0), ks[p])
+        query_sum = query_sum[0:16] * head_mask[0] + query_sum[16:32] * head_mask[1]
+        z_b[z, p : p + 1, :] = jnp.sum(query_sum, axis=0, keepdims=True) * score_scale
         z_b[z, pairs + p : pairs + p + 1, :] = jnp.sum(
-            fold_rows(dv.astype(F32)), axis=0, keepdims=True
+            fold_rows(grad_att[p].astype(F32)), axis=0, keepdims=True
         )
-
-    sum_up()
-    send_all(0, seq_size, seq, plane_a)
+    send_all(0, group, z, column_b)
     for p in range(pairs):
-        prepare(p, near_rows)
-    whole(grad_far, grad_far, gat_send.at[0], gat_recv.at[0]).wait()
-    for p in range(pairs):
-        prepare(p, far_rows)
-    score_grads(0)
-    for p in range(pairs):
-        if p + 1 < pairs:
-            score_grads(p + 1)
-        attend_back(p)
-    send_all(0, group, z, column_b)
+        attend_back(p, 0)
     wait_all(pool_a, seq_size, bias_copy(0, partner, z))
     z_a[z] = total_of(pool_a, range(seq_size))
     send_all(0, group, z, column_a)
 
-    def part_copy(c, j):
+    home_line = z - z_half * rows
+
+    def part_copy(turn, j):
         at = far_at(j)
         return remote(
-            part_out.at[c, at], part_in.at[c, at], part_send.at[c, j], part_recv.at[c, j], partner, z
+            part_out.at[turn, at],
+            part_in.at[turn, at],
+            part_send.at[turn, j],
+            part_recv.at[turn, j],
+            partner,
+            z,
         )
 
-    def token_grad(first, c):
-        mine_now = core == (1 - z_half if first else z_half)
-        at = pl.ds(pl.multiple_of(jnp.where(mine_now, half, 0), half), half)
-        columns = slice(c * GRAD_COLUMNS, (c + 1) * GRAD_COLUMNS)
-        term = dot_nt(grad_qkv[at, :], m_qkv[columns, :])
-
-        @pl.when(mine_now)
+    def token_grad(turn, which):
+        own = core == (1 - z_half if turn == 0 else z_half)
+        columns = pl.ds(pl.multiple_of(which * side, side), side)
+        term = dot_nt(grad_qkv[turn], m_qkv[columns, :])
+        return term + jnp.where(own, 1.0, 0.0) * grad_h[:, columns]
+
+    def finish(turn):
+        for j in range(half_blocks):
+            block = (1 - z_half if turn == 0 else z_half) * half_blocks + j
+            at = slice(j * span, (j + 1) * span)
+            part_copy(turn, j).wait_recv()
+            grad_out[turn, at, :] = (part[at, :] + part_in[turn, at, :].astype(F32)).astype(BF16)
+            source = grad_out.at[turn, at]
+            target_ref = grad_home.at[home_line, core]
+            stays = (block == z) & (core == z_half)
+
+            @pl.when(jnp.logical_not(stays))
+            def _():
+                remote(
+                    source,
+                    target_ref,
+                    grad_send.at[turn],
+                    grad_recv.at[home_line],
+                    base + z_half,
+                    block,
+                ).start()
+
+            @pl.when(stays)
+            def _():
+                pltpu.make_async_copy(source, target_ref, in_sem.at[3]).start()
+
+    def grads_done():
+        everything = grad_out.at[0]
+        whole(everything, everything, grad_send.at[0], grad_recv.at[0]).wait_send()
+        one = everything.at[0:span]
+
+        @pl.when(core == z_half)
         def _():
-            part[c] = term
-
-        @pl.when(jnp.logical_not(mine_now))
+            pltpu.make_async_copy(one, one, in_sem.at[3]).wait()
+            if half_blocks > 1:
+                rest = everything.at[span:half]
+                whole(rest, rest, grad_send.at[1], grad_recv.at[0]).wait_send()
+
+        @pl.when(core != z_half)
         def _():
-            for j in range(half_blocks):
-                at = slice(j * span, (j + 1) * span)
-                part_out[c, at, :] = term[at].astype(BF16)
-                part_copy(c, j).start()
-
-    home_line = z - z_half * rows
-
-    def finish(first, c):
-        columns = slice(c * GRAD_COLUMNS, (c + 1) * GRAD_COLUMNS)
-
-        @pl.when(core == (1 - z_half if first else z_half))
-        def _():
-            for j in range(half_blocks):
-                block = core * half_blocks + j
-                at = slice(j * span, (j + 1) * span)
-                part_copy(c, j).wait_recv()
-                total = grad_h[at, columns] + part[c, at, :] + part_in[c, at, :].astype(F32)
-                grad_out[c, at, :] = total.astype(BF16)
-                source = grad_out.at[c, at]
-
-                @pl.when(block != z)
-                def _():
-                    remote(
-                        source,
-                        grad_home.at[home_line, c],
-                        grad_send.at[j],
-                        grad_recv.at[home_line],
-                        base + z_half,
-                        block,
-                    ).start()
-
-                @pl.when(block == z)
-                def _():
-                    pltpu.make_async_copy(source, grad_home.at[home_line, c], in_sem.at[3]).start()
-
-    def grads_done():
-        for j in range(half_blocks):
-            block = core * half_blocks + j
-            everything = grad_home.at[home_line]
-
-            @pl.when(block != z)
-            def _():
-                whole(everything, everything, grad_send.at[j], grad_recv.at[home_line]).wait_send()
-
-            @pl.when(block == z)
-            def _():
-                pltpu.make_async_copy(everything, everything, in_sem.at[3]).wait()
+            whole(everything, everything, grad_send.at[1], grad_recv.at[0]).wait_send()
 
         for r in range(rows):
+            everything = grad_home.at[r]
 
             @pl.when(core * rows + r != z)
             def _():
-                everything = grad_home.at[r]
                 whole(everything, everything, grad_send.at[0], grad_recv.at[r]).wait_recv()
 
-    pieces = part.shape[0]
-    for first in (True, False):
-        for c in range(pieces):
-            token_grad(first, c)
-            if c >= GRAD_LAG:
-                finish(first, c - GRAD_LAG)
-        for c in range(pieces - GRAD_LAG, pieces):
-            finish(first, c)
+            @pl.when(core * rows + r == z)
+            def _():
+                one = everything.at[0]
+                whole(one, one, grad_send.at[0], grad_recv.at[r]).wait_recv()
+
+    for turn in range(2):
+        if turn == 1:
+            for p in range(pairs):
+                attend_back(p, 1)
+        part_out[turn] = token_grad(turn, far).astype(BF16)
+        for j in range(half_blocks):
+            part_copy(turn, j).start()
+        part[...] = token_grad(turn, core)
+        finish(turn)
     wait_all(z_a, group, bias_copy(1, partner, z))
     sums_a[own_slice] = total_of(z_a, range(group))
     send_all(seq - own_slice, slices, seq, gather_a)
@@ -838,9 +859,9 @@
     pool_b[seq] = total_of(z_b, range(group))
     send_all(0, seq_size, seq, plane_b)
 
-    for c in range(pieces):
+    for turn in range(2):
         for j in range(half_blocks):
-            part_copy(c, j).wait_send()
+            part_copy(turn, j).wait_send()
     wait_all(sums_a, slices, bias_copy(2, partner, z))
     wait_all(pool_b, seq_size, bias_copy(4, partner, z))
     for i in range(2):
@@ -885,8 +906,8 @@
     copies = [pltpu.make_async_copy(layer, layer_out, sems.at[0])]
     copies[0].start()
     for r in range(rows):
-        for c in range(grad.shape[1]):
-            wide[r, :, c * GRAD_COLUMNS : (c + 1) * GRAD_COLUMNS] = grad[r, c].astype(F32)
+        for c in range(2):
+            wide[r, :, c * width // 2 : (c + 1) * width // 2] = grad[r, c].astype(F32)
         copies.append(pltpu.make_async_copy(wide.at[r], input_grad.at[r], sems.at[1 + r]))
         copies[-1].start()
     pairs = sums_b.shape[1] // 2
@@ -951,7 +972,6 @@
     pairs = side // LANES
     chunks = hidden // FF_CHUNK
     slices = min(8, seq_size)
-    pieces = width // GRAD_COLUMNS
     slice_width = width // slices
     if rows * 2 != group or pairs != 4 or hidden != 4 * width or slots != FF_CHUNK:
         raise ValueError("unsupported sizes")
@@ -980,26 +1000,28 @@
         pltpu.VMEM((pairs, half, LANES), BF16),
         pltpu.VMEM((half, width), F32),
         pltpu.VMEM((half, LANES), F32),
+        pltpu.VMEM((half, LANES), F32),
         pltpu.VMEM((half, width), F32),
         pltpu.VMEM((half, width), BF16),
         pltpu.VMEM((half, width), F32),
         pltpu.VMEM((chunks // 2, slots, slots), F32),
-        pltpu.VMEM((2, half, FF_CHUNK), F32),
+        pltpu.VMEM((half, FF_CHUNK), F32),
+        pltpu.VMEM((half, FF_CHUNK), F32),
         pltpu.VMEM((half, hidden), BF16),
         pltpu.VMEM((chunks, 8, FF_CHUNK), F32),
         pltpu.VMEM((half, width), F32),
         pltpu.VMEM((half, width), BF16),
         pltpu.VMEM((pairs, slots, LANES), BF16),
         pltpu.VMEM((pairs, half, LANES), BF16),
-        pltpu.VMEM((slots, 3 * side), BF16),
+        pltpu.VMEM((2, half, 3 * side), BF16),
         pltpu.VMEM((pairs, LANES, slots), BF16),
         pltpu.VMEM((2 * pairs, slots, 2 * LANES), BF16),
         pltpu.VMEM((pairs, LANES, slots), BF16),
-        pltpu.VMEM((4, slots, slots), BF16),
-        pltpu.VMEM((pieces, half, GRAD_COLUMNS), F32),
-        pltpu.VMEM((pieces, half, GRAD_COLUMNS), BF16),
-        pltpu.VMEM((pieces, half, GRAD_COLUMNS), BF16),
-        pltpu.VMEM((pieces, half, GRAD_COLUMNS), BF16),
+        pltpu.VMEM((2 * pairs, slots, slots), BF16),
+        pltpu.VMEM((half, side), F32),
+        pltpu.VMEM((2, half, side), BF16),
+        pltpu.VMEM((2, half, side), BF16),
+        pltpu.VMEM((2, half, side), BF16),
         pltpu.VMEM((half, width), BF16),
         pltpu.VMEM((8, width), F32),
         pltpu.VMEM((seq_size, 8, slice_width), F32),
@@ -1021,9 +1043,9 @@
         dma((1,)),
         dma((half_blocks,)),
         dma((rows,)),
-        dma((pieces, half_blocks)),
-        dma((pieces, half_blocks)),
-        dma((half_blocks,)),
+        dma((2, half_blocks)),
+        dma((2, half_blocks)),
+        dma((2,)),
         dma((rows,)),
         dma((5,)),
         dma((5,)),
@@ -1043,7 +1065,7 @@
         functools.partial(kernel, seq_size, group),
         out_shape=(
             pltpu.VMEM(tokens.shape, BF16),
-            pltpu.VMEM((rows, pieces, span, GRAD_COLUMNS), BF16),
+            pltpu.VMEM((rows, 2, span, side), BF16),
             pltpu.VMEM((slices, 8, slice_width), F32),
             pltpu.VMEM((2, 8, LANES), F32),
         ),

time: 58.4 us -> 56.5 us (0.967)
  Pallas kernels: 57.1 us -> 54.8 us
    pallas_call x1, Pallas kernels: 55.9 us -> 53.6 us  [per_device(): pl.pallas_call(functools.partial(kernel, seq_size, group), out_shape=(plt...]
where the time goes in v4:
time: 56.5 us; the launch traced here: 55.6 us
  Pallas kernels  54.8 us (97%)
  between operations  0.82 us (1%)
    pallas_call x1, Pallas kernels, per_device(): pl.pallas_call(functools.partial(kernel, seq_size, group), out_shape=(plt...  53.6 us
    pallas_call x1, Pallas kernels, per_device(): pl.pallas_call(finish_kernel, out_shape=(jax.ShapeDtypeStruct(tokens.shap...  1.24 us

profile of v4, /device:TPU:0, one launch (start us, length us, event | category | flops | bytes accessed | tf_op | source)
XLA Modules:
  0.0 55.6 jit_solution(10360316514896005829)
XLA Ops:
  0.7 53.6 %shard_map.250 = (bf16[2,128,1024]{2,1,0:T(8,128)(2,1)S(1)}, bf16[2,2,128,512]{3,2,1,0:T(8,128)(2,1)S(1)}, f32[8,8,128]{2,1,0:T(8,128)S(1)}, f32[2,8,128]{2,1,0:T(8,128)S(1)}) custom-call(bf16[2,128,1024]{2,1,0:T(8,128)(2,1)} %tokens.1, bf16[2,128,1024]{2,1,0:T(8,128)(2,1)} %cotangent.1, s32[2,3]{1,0:T(2,128)} %doc_lengths.1, s32[2]{0:T(128)} %pad_counts.1, ...), custom_call_target="tpu_custom_call" | custom-call | tf_op jit(solution)/shard_map/pallas_call | solution.py:1064
  54.2 1.2 %shard_map.251 = (bf16[2,128,1024]{2,1,0:T(8,128)(2,1)}, f32[2,128,1024]{2,1,0:T(8,128)}, f32[1,1024]{1,0:T(1,128)}, f32[1,1024]{1,0:T(1,128)}, f32[1,1024]{1,0:...) custom-call(bf16[2,128,1024]{2,1,0:T(8,128)(2,1)S(1)} %get-tuple-element.22.layer, ...), custom_call_target="tpu_custom_call" | custom-call | tf_op jit(solution)/shard_map/pallas_call | solution.py:1092

commit v5 on v4

--- a/solution.py
+++ b/solution.py
@@ -80,6 +80,7 @@
     sums_a,
     sums_b,
     m_qkv,
+    turned_qkv,
     m_out,
     m_inner,
     m_outer,
@@ -325,6 +326,11 @@
     send_tokens()
     keep(tokens, row, tok_at, in_sem.at[0])
     keep(cotangent, cot, cot_at, in_sem.at[1])
+
+    @pl.when(early)
+    def _():
+        send_cotangents()
+
     pltpu.make_async_copy(w_out.at[mine], m_out.at[0:side], w_sem.at[1]).start()
     pltpu.make_async_copy(w_out.at[theirs], m_out.at[side:width], w_sem.at[1]).start()
     for f in range(chunks):
@@ -369,6 +375,8 @@
         for p in range(pairs):
             cut = slice(p * LANES, (p + 1) * LANES)
             qs[p, at, :] = q[:, cut].astype(BF16)
+            if span % LANES == 0:
+                turned[p, :, at] = q[:, cut].astype(BF16).T
             ks[p, at, :] = k[:, cut].astype(BF16)
             vs[p, at, :] = v[:, cut].astype(BF16)
 
@@ -382,13 +390,14 @@
         @pl.when(own)
         def _():
             block = core * half_blocks + j
-            arrived(tokens, row, near_at(j), block, tok_send, tok_recv, in_sem.at[0])
-            pass_on(j).start()
 
             @pl.when((i == group - 1) & jnp.logical_not(early))
             def _():
                 send_cotangents()
 
+            arrived(tokens, row, near_at(j), block, tok_send, tok_recv, in_sem.at[0])
+            pass_on(j).start()
+
         @pl.when(jnp.logical_not(own))
         def _():
             pass_on(j).wait_recv()
@@ -399,6 +408,9 @@
 
         project(pl.ds(pl.multiple_of(jnp.where(own, half, 0) + j * span, span), span))
         return carry
+
+    for i in range(0, 3 * side, 2 * LANES):
+        turned_qkv[i : i + 2 * LANES, :] = m_qkv[:, i : i + 2 * LANES].T
 
     lax.fori_loop(0, group, project_step, 0)
 
@@ -457,12 +469,6 @@
             )
             att_copy.start()
 
-            @pl.when(early)
-            def _():
-                tokens_sent()
-                send_cotangents()
-
-
     def whole(source, target, send_sem, recv_sem):
         return remote(source, target, send_sem, recv_sem, partner, z)
 
@@ -583,8 +589,9 @@
         home_block(
             core * half_blocks + j, layer_out, layer_home, lay_send, lay_recv, in_sem.at[2]
         )
-    for p in range(pairs):
-        turned[p] = qs[p].T
+    if span % LANES != 0:
+        for p in range(pairs):
+            turned[p] = qs[p].T
 
     def cot_wait(j, carry):
         at = pl.ds(pl.multiple_of(j * span, span), span)
@@ -721,9 +728,16 @@
         grad_scores[head, at, :] = grads.astype(BF16)
         return fold_rows(grads)
 
+    quarter = slots // 4
+
+    def half_of(turn):
+        return 1 - z_half if turn < 2 else z_half
+
+    def start_of(turn):
+        return jnp.where(core == half_of(turn), half, 0) + turn % 2 * quarter
+
     def attend_back(p, turn):
-        start = jnp.where(core == (1 - z_half if turn == 0 else z_half), half, 0)
-        part_of = pl.ds(pl.multiple_of(start, half), half)
+        part_of = pl.ds(pl.multiple_of(start_of(turn), quarter), quarter)
         dq = None
         dk = []
         dv = []
@@ -773,30 +787,25 @@
 
     home_line = z - z_half * rows
 
-    def part_copy(turn, j):
-        at = far_at(j)
+    def part_copy(turn):
         return remote(
-            part_out.at[turn, at],
-            part_in.at[turn, at],
-            part_send.at[turn, j],
-            part_recv.at[turn, j],
-            partner,
-            z,
+            part_out.at[turn], part_in.at[turn], part_send.at[turn], part_recv.at[turn], partner, z
         )
 
     def token_grad(turn, which):
-        own = core == (1 - z_half if turn == 0 else z_half)
+        own = core == half_of(turn)
         columns = pl.ds(pl.multiple_of(which * side, side), side)
-        term = dot_nt(grad_qkv[turn], m_qkv[columns, :])
-        return term + jnp.where(own, 1.0, 0.0) * grad_h[:, columns]
+        near = slice(turn % 2 * quarter, (turn % 2 + 1) * quarter)
+        term = dot(grad_qkv[turn], turned_qkv[:, columns])
+        return term + jnp.where(own, 1.0, 0.0) * grad_h[near, columns]
 
     def finish(turn):
-        for j in range(half_blocks):
-            block = (1 - z_half if turn == 0 else z_half) * half_blocks + j
-            at = slice(j * span, (j + 1) * span)
-            part_copy(turn, j).wait_recv()
-            grad_out[turn, at, :] = (part[at, :] + part_in[turn, at, :].astype(F32)).astype(BF16)
-            source = grad_out.at[turn, at]
+        part_copy(turn).wait_recv()
+        at = slice(turn * quarter, (turn + 1) * quarter)
+        grad_out[at, :] = (part[turn % 2] + part_in[turn].astype(F32)).astype(BF16)
+        for j in range(quarter // span):
+            block = half_of(turn) * half_blocks + turn % 2 * (quarter // span) + j
+            source = grad_out.at[turn * quarter + j * span : turn * quarter + (j + 1) * span]
             target_ref = grad_home.at[home_line, core]
             stays = (block == z) & (core == z_half)
 
@@ -805,7 +814,7 @@
                 remote(
                     source,
                     target_ref,
-                    grad_send.at[turn],
+                    grad_send.at[0],
                     grad_recv.at[home_line],
                     base + z_half,
                     block,
@@ -816,20 +825,16 @@
                 pltpu.make_async_copy(source, target_ref, in_sem.at[3]).start()
 
     def grads_done():
-        everything = grad_out.at[0]
-        whole(everything, everything, grad_send.at[0], grad_recv.at[0]).wait_send()
-        one = everything.at[0:span]
-
         @pl.when(core == z_half)
         def _():
+            one = grad_out.at[0:span]
+            rest = grad_out.at[span:slots]
             pltpu.make_async_copy(one, one, in_sem.at[3]).wait()
-            if half_blocks > 1:
-                rest = everything.at[span:half]
-                whole(rest, rest, grad_send.at[1], grad_recv.at[0]).wait_send()
+            whole(rest, rest, grad_send.at[0], grad_recv.at[0]).wait_send()
 
         @pl.when(core != z_half)
         def _():
-            whole(everything, everything, grad_send.at[1], grad_recv.at[0]).wait_send()
+            whole(grad_out, grad_out, grad_send.at[0], grad_recv.at[0]).wait_send()
 
         for r in range(rows):
             everything = grad_home.at[r]
@@ -843,15 +848,15 @@
                 one = everything.at[0]
                 whole(one, one, grad_send.at[0], grad_recv.at[r]).wait_recv()
 
-    for turn in range(2):
-        if turn == 1:
+    for turn in range(4):
+        if turn > 0:
             for p in range(pairs):
-                attend_back(p, 1)
+                attend_back(p, turn)
+            finish(turn - 1)
         part_out[turn] = token_grad(turn, far).astype(BF16)
-        for j in range(half_blocks):
-            part_copy(turn, j).start()
-        part[...] = token_grad(turn, core)
-        finish(turn)
+        part_copy(turn).start()
+        part[turn % 2] = token_grad(turn, core)
+    finish(3)
     wait_all(z_a, group, bias_copy(1, partner, z))
     sums_a[own_slice] = total_of(z_a, range(group))
     send_all(seq - own_slice, slices, seq, gather_a)
@@ -859,18 +864,13 @@
     pool_b[seq] = total_of(z_b, range(group))
     send_all(0, seq_size, seq, plane_b)
 
-    for turn in range(2):
-        for j in range(half_blocks):
-            part_copy(turn, j).wait_send()
+    for turn in range(4):
+        part_copy(turn).wait_send()
     wait_all(sums_a, slices, bias_copy(2, partner, z))
     wait_all(pool_b, seq_size, bias_copy(4, partner, z))
     for i in range(2):
         sums_b[i] = total_of(pool_b, range(i, seq_size, 2))
-
-    @pl.when(jnp.logical_not(early))
-    def _():
-        tokens_sent()
-
+    tokens_sent()
     cotangents_sent()
 
     def pass_wait(j, carry):
@@ -972,8 +972,9 @@
     pairs = side // LANES
     chunks = hidden // FF_CHUNK
     slices = min(8, seq_size)
+    quarter = slots // 4
     slice_width = width // slices
-    if rows * 2 != group or pairs != 4 or hidden != 4 * width or slots != FF_CHUNK:
+    if rows * 2 != group or pairs != 4 or hidden != 4 * width or slots != FF_CHUNK or quarter % span != 0:
         raise ValueError("unsupported sizes")
 
     any_space = pl.BlockSpec(memory_space=pl.ANY)
@@ -982,6 +983,7 @@
     dma = pltpu.SemaphoreType.DMA
     scratch = [
         pltpu.VMEM((width, 3 * side), BF16),
+        pltpu.VMEM((3 * side, width), BF16),
         pltpu.VMEM((width, width), BF16),
         pltpu.VMEM((chunks, width, FF_CHUNK), BF16),
         pltpu.VMEM((hidden, width), BF16),
@@ -1013,15 +1015,15 @@
         pltpu.VMEM((half, width), BF16),
         pltpu.VMEM((pairs, slots, LANES), BF16),
         pltpu.VMEM((pairs, half, LANES), BF16),
-        pltpu.VMEM((2, half, 3 * side), BF16),
+        pltpu.VMEM((4, quarter, 3 * side), BF16),
         pltpu.VMEM((pairs, LANES, slots), BF16),
         pltpu.VMEM((2 * pairs, slots, 2 * LANES), BF16),
         pltpu.VMEM((pairs, LANES, slots), BF16),
         pltpu.VMEM((2 * pairs, slots, slots), BF16),
-        pltpu.VMEM((half, side), F32),
-        pltpu.VMEM((2, half, side), BF16),
-        pltpu.VMEM((2, half, side), BF16),
-        pltpu.VMEM((2, half, side), BF16),
+        pltpu.VMEM((2, quarter, side), F32),
+        pltpu.VMEM((4, quarter, side), BF16),
+        pltpu.VMEM((4, quarter, side), BF16),
+        pltpu.VMEM((slots, side), BF16),
         pltpu.VMEM((half, width), BF16),
         pltpu.VMEM((8, width), F32),
         pltpu.VMEM((seq_size, 8, slice_width), F32),
@@ -1043,9 +1045,9 @@
         dma((1,)),
         dma((half_blocks,)),
         dma((rows,)),
-        dma((2, half_blocks)),
-        dma((2, half_blocks)),
-        dma((2,)),
+        dma((4,)),
+        dma((4,)),
+        dma((1,)),
         dma((rows,)),
         dma((5,)),
         dma((5,)),

time: 56.5 us -> 55 us (0.973)
  Pallas kernels: 54.8 us -> 53.1 us
    pallas_call x1, Pallas kernels: 53.6 us -> 51.9 us  [per_device(): pl.pallas_call(functools.partial(kernel, seq_size, group), out_shape=(plt...]
where the time goes in v5:
time: 55 us; the launch traced here: 53.9 us
  Pallas kernels  53.1 us (97%)
  between operations  0.82 us (1%)
    pallas_call x1, Pallas kernels, per_device(): pl.pallas_call(functools.partial(kernel, seq_size, group), out_shape=(plt...  51.9 us
    pallas_call x1, Pallas kernels, per_device(): pl.pallas_call(finish_kernel, out_shape=(jax.ShapeDtypeStruct(tokens.shap...  1.24 us

profile of v5, /device:TPU:0, one launch (start us, length us, event | category | flops | bytes accessed | tf_op | source)
XLA Modules:
  0.0 53.9 jit_solution(1401801232356323528)
XLA Ops:
  0.7 51.9 %shard_map.250 = (bf16[2,128,1024]{2,1,0:T(8,128)(2,1)S(1)}, bf16[2,2,128,512]{3,2,1,0:T(8,128)(2,1)S(1)}, f32[8,8,128]{2,1,0:T(8,128)S(1)}, f32[2,8,128]{2,1,0:T(8,128)S(1)}) custom-call(bf16[2,128,1024]{2,1,0:T(8,128)(2,1)} %tokens.1, bf16[2,128,1024]{2,1,0:T(8,128)(2,1)} %cotangent.1, s32[2,3]{1,0:T(2,128)} %doc_lengths.1, s32[2]{0:T(128)} %pad_counts.1, ...), custom_call_target="tpu_custom_call" | custom-call | tf_op jit(solution)/shard_map/pallas_call | solution.py:1066
  52.5 1.2 %shard_map.251 = (bf16[2,128,1024]{2,1,0:T(8,128)(2,1)}, f32[2,128,1024]{2,1,0:T(8,128)}, f32[1,1024]{1,0:T(1,128)}, f32[1,1024]{1,0:T(1,128)}, f32[1,1024]{1,0:...) custom-call(bf16[2,128,1024]{2,1,0:T(8,128)(2,1)S(1)} %get-tuple-element.22.layer, ...), custom_call_target="tpu_custom_call" | custom-call | tf_op jit(solution)/shard_map/pallas_call | solution.py:1094

commit v6 on v5

--- a/solution.py
+++ b/solution.py
@@ -200,6 +200,9 @@
         )
         return carry
 
+    for step in range(group - 1, 0, -1):
+        greet_z(step, 0)
+
     for r in range(half_blocks):
         other = core * half_blocks + r
 
@@ -208,7 +211,6 @@
             pl.semaphore_signal(barrier, inc=1, device_id=(partner, other), device_id_type=MESH)
 
     lax.fori_loop(1, seq_size, greet_seq, 0)
-    lax.fori_loop(1, group, greet_z, 0)
 
     mine = pl.ds(pl.multiple_of(core * side, side), side)
     theirs = pl.ds(pl.multiple_of(far * side, side), side)
@@ -383,15 +385,16 @@
 
     def project_step(i, carry):
         in_turn = core == z_half
-        own = jnp.where(in_turn, i < half_blocks, lax.rem(i, 2) == 1)
-        step = jnp.where(in_turn, lax.rem(i, half_blocks), i // 2)
+        own = jnp.where(in_turn, i < half_blocks, (i >= 1) & (i <= half_blocks))
+        passed = jnp.where(i == 0, 0, i - half_blocks)
+        step = jnp.where(in_turn, lax.rem(i, half_blocks), jnp.where(own, i - 1, passed))
         j = taken(jnp.where(own, core, far), step)
 
         @pl.when(own)
         def _():
             block = core * half_blocks + j
 
-            @pl.when((i == group - 1) & jnp.logical_not(early))
+            @pl.when((i == half_blocks) & jnp.logical_not(early))
             def _():
                 send_cotangents()
 
@@ -500,9 +503,12 @@
     def activate(f):
         columns = slice(f * FF_CHUNK, (f + 1) * FF_CHUNK)
         inner = raw[f % 2][...] + bias_inner[:, columns]
-        cdf = 0.5 * (1.0 + lax.erf(inner * 0.7071067811865476))
+        scaled = inner * 0.7071067811865476
+        cdf = 0.5 + 0.5 * lax.erf(scaled)
         which, lines = slope_at(f)
-        slope[which, lines, :] = cdf + inner * jnp.exp(-0.5 * inner * inner) * 0.3989422804014327
+        slope[which, lines, :] = cdf + scaled * 0.5641895835477563 * jnp.exp2(
+            scaled * scaled * -1.4426950408889634
+        )
         active[:, columns] = (inner * cdf).astype(BF16)
 
     raw = (raw_even, raw_odd)
@@ -781,9 +787,6 @@
     send_all(0, group, z, column_b)
     for p in range(pairs):
         attend_back(p, 0)
-    wait_all(pool_a, seq_size, bias_copy(0, partner, z))
-    z_a[z] = total_of(pool_a, range(seq_size))
-    send_all(0, group, z, column_a)
 
     home_line = z - z_half * rows
 
@@ -856,6 +859,10 @@
         part_out[turn] = token_grad(turn, far).astype(BF16)
         part_copy(turn).start()
         part[turn % 2] = token_grad(turn, core)
+        if turn == 0:
+            wait_all(pool_a, seq_size, bias_copy(0, partner, z))
+            z_a[z] = total_of(pool_a, range(seq_size))
+            send_all(0, group, z, column_a)
     finish(3)
     wait_all(z_a, group, bias_copy(1, partner, z))
     sums_a[own_slice] = total_of(z_a, range(group))

time: 55 us -> 55 us (level)
  the two profiles are of different devices: /device:TPU:0 before, /device:TPU:9 now
where the time goes in v6:
time: 55 us; the launch traced here: 54.8 us
  Pallas kernels  54 us (98%)
  between operations  0.82 us (1%)
    pallas_call x1, Pallas kernels, per_device(): pl.pallas_call(functools.partial(kernel, seq_size, group), out_shape=(plt...  52.7 us
    pallas_call x1, Pallas kernels, per_device(): pl.pallas_call(finish_kernel, out_shape=(jax.ShapeDtypeStruct(tokens.shap...  1.24 us

profile of v6, /device:TPU:9, one launch (start us, length us, event | category | flops | bytes accessed | tf_op | source)
XLA Modules:
  0.0 54.8 jit_solution(10249995470142070067)
XLA Ops:
  0.7 52.7 %shard_map.250 = (bf16[2,128,1024]{2,1,0:T(8,128)(2,1)S(1)}, bf16[2,2,128,512]{3,2,1,0:T(8,128)(2,1)S(1)}, f32[8,8,128]{2,1,0:T(8,128)S(1)}, f32[2,8,128]{2,1,0:T(8,128)S(1)}) custom-call(bf16[2,128,1024]{2,1,0:T(8,128)(2,1)} %tokens.1, bf16[2,128,1024]{2,1,0:T(8,128)(2,1)} %cotangent.1, s32[2,3]{1,0:T(2,128)} %doc_lengths.1, s32[2]{0:T(128)} %pad_counts.1, ...), custom_call_target="tpu_custom_call" | custom-call | tf_op jit(solution)/shard_map/pallas_call | solution.py:1073
  53.4 1.2 %shard_map.251 = (bf16[2,128,1024]{2,1,0:T(8,128)(2,1)}, f32[2,128,1024]{2,1,0:T(8,128)}, f32[1,1024]{1,0:T(1,128)}, f32[1,1024]{1,0:T(1,128)}, f32[1,1024]{1,0:...) custom-call(bf16[2,128,1024]{2,1,0:T(8,128)(2,1)S(1)} %get-tuple-element.22.layer, ...), custom_call_target="tpu_custom_call" | custom-call | tf_op jit(solution)/shard_map/pallas_call | solution.py:1101

commit v7 on v6

--- a/solution.py
+++ b/solution.py
@@ -117,6 +117,7 @@
     lefts,
     grads_turned,
     grad_scores,
+    score_sums,
     part,
     part_out,
     part_in,
@@ -309,6 +310,9 @@
     tok_at = near_at(z - z_half * half_blocks)
     cot_at = pl.ds(pl.multiple_of((z - z_half * half_blocks) * span, span), span)
 
+    gives_way = jnp.logical_not(early) & (core == z_half)
+    goes_far = jnp.logical_not(early) & (core != z_half)
+
     def send_tokens():
         for index in range(rows):
             spread(index, tokens, row, tok_at, tok_send, tok_recv)
@@ -325,7 +329,10 @@
         for index in range(rows):
             spread_done(index, cotangent, cot, cot_at, cot_send, cot_recv)
 
-    send_tokens()
+    @pl.when(jnp.logical_not(goes_far))
+    def _():
+        send_tokens()
+
     keep(tokens, row, tok_at, in_sem.at[0])
     keep(cotangent, cot, cot_at, in_sem.at[1])
 
@@ -414,6 +421,10 @@
 
     for i in range(0, 3 * side, 2 * LANES):
         turned_qkv[i : i + 2 * LANES, :] = m_qkv[:, i : i + 2 * LANES].T
+
+    @pl.when(goes_far)
+    def _():
+        send_tokens()
 
     lax.fori_loop(0, group, project_step, 0)
 
@@ -591,13 +602,15 @@
                     target,
                 ).wait_recv()
 
-    for j in range(half_blocks):
-        home_block(
-            core * half_blocks + j, layer_out, layer_home, lay_send, lay_recv, in_sem.at[2]
-        )
-    if span % LANES != 0:
-        for p in range(pairs):
-            turned[p] = qs[p].T
+    def send_layer_out():
+        for j in range(half_blocks):
+            home_block(
+                core * half_blocks + j, layer_out, layer_home, lay_send, lay_recv, in_sem.at[2]
+            )
+
+    @pl.when(jnp.logical_not(gives_way))
+    def _():
+        send_layer_out()
 
     def cot_wait(j, carry):
         at = pl.ds(pl.multiple_of(j * span, span), span)
@@ -635,6 +648,10 @@
             )
             total = term if total is None else total + term
         acc[:, n : n + FEATURE_CHUNK] = total
+    @pl.when(gives_way)
+    def _():
+        send_layer_out()
+
     def norm_first_back(step, carry):
         beta_sum, out_sum = carry
         at = lines_of(step)
@@ -739,8 +756,15 @@
     def half_of(turn):
         return 1 - z_half if turn < 2 else z_half
 
+    home_quarter = (z - z_half * half_blocks) * span // quarter
+
+    def quarter_of(turn):
+        if turn < 2:
+            return turn
+        return 1 - home_quarter if turn == 2 else home_quarter
+
     def start_of(turn):
-        return jnp.where(core == half_of(turn), half, 0) + turn % 2 * quarter
+        return jnp.where(core == half_of(turn), half, 0) + quarter_of(turn) * quarter
 
     def attend_back(p, turn):
         part_of = pl.ds(pl.multiple_of(start_of(turn), quarter), quarter)
@@ -761,30 +785,31 @@
             grad_qkv[turn, :, i * side + p * LANES : i * side + (p + 1) * LANES] = block
 
     def score_grads_of(at):
-        sums = []
         prepare(0, at)
         for p in range(pairs):
             if p + 1 < pairs:
                 prepare(p + 1, at)
-            sums += [score_grads(2 * p, at), score_grads(2 * p + 1, at)]
-        return sums
-
-    near_sums = score_grads_of(near_rows)
+            for head in (2 * p, 2 * p + 1):
+                sums = score_grads(head, at)
+                score_sums[head] = sums if at == near_rows else score_sums[head] + sums
+
+    def sum_up_heads():
+        for p in range(pairs):
+            rows_of_pair = []
+            for head in (2 * p, 2 * p + 1):
+                sums = score_sums[head]
+                high = sums.astype(BF16)
+                rows_of_pair += [high, (sums - high.astype(F32)).astype(BF16)]
+            query_sum = dot(jnp.concatenate(rows_of_pair, axis=0), ks[p])
+            query_sum = query_sum[0:16] * head_mask[0] + query_sum[16:32] * head_mask[1]
+            z_b[z, p : p + 1, :] = jnp.sum(query_sum, axis=0, keepdims=True) * score_scale
+            z_b[z, pairs + p : pairs + p + 1, :] = jnp.sum(
+                fold_rows(grad_att[p].astype(F32)), axis=0, keepdims=True
+            )
+
+    score_grads_of(near_rows)
     whole(grad_far, grad_far, gat_send.at[0], gat_recv.at[0]).wait()
-    far_sums = score_grads_of(far_rows)
-    for p in range(pairs):
-        rows_of_pair = []
-        for head in (2 * p, 2 * p + 1):
-            sums = near_sums[head] + far_sums[head]
-            high = sums.astype(BF16)
-            rows_of_pair += [high, (sums - high.astype(F32)).astype(BF16)]
-        query_sum = dot(jnp.concatenate(rows_of_pair, axis=0), ks[p])
-        query_sum = query_sum[0:16] * head_mask[0] + query_sum[16:32] * head_mask[1]
-        z_b[z, p : p + 1, :] = jnp.sum(query_sum, axis=0, keepdims=True) * score_scale
-        z_b[z, pairs + p : pairs + p + 1, :] = jnp.sum(
-            fold_rows(grad_att[p].astype(F32)), axis=0, keepdims=True
-        )
-    send_all(0, group, z, column_b)
+    score_grads_of(far_rows)
     for p in range(pairs):
         attend_back(p, 0)
 
@@ -798,7 +823,7 @@
     def token_grad(turn, which):
         own = core == half_of(turn)
         columns = pl.ds(pl.multiple_of(which * side, side), side)
-        near = slice(turn % 2 * quarter, (turn % 2 + 1) * quarter)
+        near = pl.ds(pl.multiple_of(quarter_of(turn) * quarter, quarter), quarter)
         term = dot(grad_qkv[turn], turned_qkv[:, columns])
         return term + jnp.where(own, 1.0, 0.0) * grad_h[near, columns]
 
@@ -807,7 +832,7 @@
         at = slice(turn * quarter, (turn + 1) * quarter)
         grad_out[at, :] = (part[turn % 2] + part_in[turn].astype(F32)).astype(BF16)
         for j in range(quarter // span):
-            block = half_of(turn) * half_blocks + turn % 2 * (quarter // span) + j
+            block = half_of(turn) * half_blocks + quarter_of(turn) * (quarter // span) + j
             source = grad_out.at[turn * quarter + j * span : turn * quarter + (j + 1) * span]
             target_ref = grad_home.at[home_line, core]
             stays = (block == z) & (core == z_half)
@@ -855,14 +880,18 @@
         if turn > 0:
             for p in range(pairs):
                 attend_back(p, turn)
+        if turn > 1:
             finish(turn - 1)
         part_out[turn] = token_grad(turn, far).astype(BF16)
         part_copy(turn).start()
         part[turn % 2] = token_grad(turn, core)
         if turn == 0:
+            sum_up_heads()
+            send_all(0, group, z, column_b)
             wait_all(pool_a, seq_size, bias_copy(0, partner, z))
             z_a[z] = total_of(pool_a, range(seq_size))
             send_all(0, group, z, column_a)
+            finish(0)
     finish(3)
     wait_all(z_a, group, bias_copy(1, partner, z))
     sums_a[own_slice] = total_of(z_a, range(group))
@@ -1027,6 +1056,7 @@
         pltpu.VMEM((2 * pairs, slots, 2 * LANES), BF16),
         pltpu.VMEM((pairs, LANES, slots), BF16),
         pltpu.VMEM((2 * pairs, slots, slots), BF16),
+        pltpu.VMEM((2 * pairs, 8, slots), F32),
         pltpu.VMEM((2, quarter, side), F32),
         pltpu.VMEM((4, quarter, side), BF16),
         pltpu.VMEM((4, quarter, side), BF16),

time: 55 us -> 57.2 us (1.040)
  the two profiles are of different devices: /device:TPU:9 before, /device:TPU:0 now
where the time goes in v7:
time: 57.2 us; the launch traced here: 57 us
  Pallas kernels  56.2 us (98%)
  between operations  0.82 us (1%)
    pallas_call x1, Pallas kernels, per_device(): pl.pallas_call(functools.partial(kernel, seq_size, group), out_shape=(plt...  55 us
    pallas_call x1, Pallas kernels, per_device(): pl.pallas_call(finish_kernel, out_shape=(jax.ShapeDtypeStruct(tokens.shap...  1.24 us

profile of v7, /device:TPU:0, one launch (start us, length us, event | category | flops | bytes accessed | tf_op | source)
XLA Modules:
  0.0 57.0 jit_solution(838581669227184772)
XLA Ops:
  0.7 55.0 %shard_map.250 = (bf16[2,128,1024]{2,1,0:T(8,128)(2,1)S(1)}, bf16[2,2,128,512]{3,2,1,0:T(8,128)(2,1)S(1)}, f32[8,8,128]{2,1,0:T(8,128)S(1)}, f32[2,8,128]{2,1,0:T(8,128)S(1)}) custom-call(bf16[2,128,1024]{2,1,0:T(8,128)(2,1)} %tokens.1, bf16[2,128,1024]{2,1,0:T(8,128)(2,1)} %cotangent.1, s32[2,3]{1,0:T(2,128)} %doc_lengths.1, s32[2]{0:T(128)} %pad_counts.1, ...), custom_call_target="tpu_custom_call" | custom-call | tf_op jit(solution)/shard_map/pallas_call | solution.py:1103
  55.6 1.2 %shard_map.251 = (bf16[2,128,1024]{2,1,0:T(8,128)(2,1)}, f32[2,128,1024]{2,1,0:T(8,128)}, f32[1,1024]{1,0:T(1,128)}, f32[1,1024]{1,0:T(1,128)}, f32[1,1024]{1,0:...) custom-call(bf16[2,128,1024]{2,1,0:T(8,128)(2,1)S(1)} %get-tuple-element.22.layer, ...), custom_call_target="tpu_custom_call" | custom-call | tf_op jit(solution)/shard_map/pallas_call | solution.py:1131
